TPU v7x, 32 devices: a whole 2x2x4 slice. The times are simulated.
32 devices in a mesh: dp: 8 (over z, x), seq: 4 (over y, core).
Axes of the slice: x: 2, y: 2, z: 4, core: 2. Of those that a mesh axis runs over, the one named last changes fastest.
Arguments:
- hidden_in: bfloat16 [16384, 640], P(('dp', 'seq')), may hold values from -6 to 6
- cotangent: bfloat16 [16384, 640], P(('dp', 'seq')), may hold values from -6 to 6
- seg_ids: int32 [8, 2048], P('dp'), may hold values from 0 to 2, as said below
- positions: int32 [8, 2048], P('dp'), may hold values from 0 to 2559, as said below
- norm_gains: bfloat16 [3072], P(('dp', 'seq')), may hold values from 0.25 to 1.75
- w_qkv: bfloat16 [640, 1536], P(None, ('dp', 'seq')), may hold values from -0.25 to 0.25
- w_out: bfloat16 [1024, 640], P(('dp', 'seq')), may hold values from -0.1875 to 0.1875
- w_gate_up: bfloat16 [640, 4096], P(None, ('dp', 'seq')), may hold values from -0.25 to 0.25
- w_down: bfloat16 [2048, 640], P(('dp', 'seq')), may hold values from -0.125 to 0.125
Outputs:
- output: bfloat16 [16384, 640], P(('dp', 'seq'))
- input_grad: float32 [16384, 640], P(('dp', 'seq'))
- gain_grad: float32 [3072], P(('dp', 'seq'))
- qkv_grad: float32 [640, 1536], P(None, ('dp', 'seq'))
- out_proj_grad: float32 [1024, 640], P(('dp', 'seq'))
- gate_up_grad: float32 [640, 4096], P(None, ('dp', 'seq'))
- down_grad: float32 [2048, 640], P(('dp', 'seq'))
Inputs may be any that keep to these rules, and one draw needn't show every extreme that they name: `seg_ids`: along a row of 2048 tokens the ids never fall, so each id covers consecutive tokens; one id covers tokens on every device of its group. `positions`: positions rise by one from each token to the next token with the same id; in every group the tokens of the first id end at position 2559.
All inputs are finite; a program needn't handle non-finite values.
Results may differ from a plain program's by a relative error of at most 0.015.
Values may be sent and summed in bfloat16 or wider, within the bound.
A program may use at most 128 MiB of HBM per device.

v0:
```python
import jax
import jax.numpy as jnp
from jax import lax
from jax.sharding import PartitionSpec as P

D = 640
H = 4
HD = 256
FF = 2048
WINDOW = 512


NORM_EPS = 1e-06
MASKED_OUT = -1e30


def from_behind(block, axis, distance):
    devices = range(lax.axis_size(axis))
    route = [(i - distance, i) for i in devices if i - distance in devices]
    return lax.ppermute(block, axis, route)


def norm_forward(values):
    inverse = lax.rsqrt(jnp.mean(values * values, -1, keepdims=True) + NORM_EPS)
    return (values * inverse, inverse)


def norm_back(normed, inverse, grad_normed):
    return inverse * (grad_normed - normed * jnp.mean(grad_normed * normed, -1, keepdims=True))


def turn_angles(pos_vals):
    half_dim = HD // 2
    inverse_freq = jnp.power(10000.0, -(2.0 * jnp.arange(half_dim, dtype=jnp.float32)) / HD)
    return pos_vals.astype(jnp.float32)[:, None] * inverse_freq[None, :]


def rope_turn(values, angles):
    half_dim = values.shape[-1] // 2
    first_half = values[..., :half_dim]
    second_half = values[..., half_dim:]
    cosine = jnp.cos(angles)
    sine_val = jnp.sin(angles)
    return jnp.concatenate(
        [
            first_half * cosine - second_half * sine_val,
            second_half * cosine + first_half * sine_val,
        ],
        -1,
    )


def rope_back(grads, angles):
    half_dim = grads.shape[-1] // 2
    first_half = grads[..., :half_dim]
    second_half = grads[..., half_dim:]
    cosine = jnp.cos(angles)
    sine_val = jnp.sin(angles)
    return jnp.concatenate(
        [
            first_half * cosine + second_half * sine_val,
            second_half * cosine - first_half * sine_val,
        ],
        -1,
    )


def split_gains(gain_vec):
    return (
        gain_vec[0:D],
        gain_vec[D : 2 * D],
        gain_vec[2 * D : 3 * D],
        gain_vec[3 * D : 4 * D],
        gain_vec[4 * D : 4 * D + HD],
        gain_vec[4 * D + HD : 4 * D + 2 * HD],
    )


def body(hidden_in, cotangent, seg_ids, positions, norm_gains, w_qkv, w_out, w_gate_up, w_down):
    row_count = hidden_in.shape[0]
    seq_count = lax.axis_size("seq")
    seq_place = lax.axis_index("seq")
    reach_count = min(seq_count - 1, (WINDOW + row_count - 2) // row_count)
    query_scale = HD ** (-0.5)
    gain_parts, qkv_full, out_full = (
        lax.all_gather(norm_gains, ("dp", "seq"), axis=0, tiled=True),
        lax.all_gather(w_qkv, ("dp", "seq"), axis=1, tiled=True),
        lax.all_gather(w_out, ("dp", "seq"), axis=0, tiled=True),
    )
    gate_up_full, down_full = (
        lax.all_gather(w_gate_up, ("dp", "seq"), axis=1, tiled=True),
        lax.all_gather(w_down, ("dp", "seq"), axis=0, tiled=True),
    )
    gain_in, gain_attn_post, gain_ffn_pre, gain_ffn_post, gain_query, gain_key = split_gains(
        gain_parts.astype(jnp.float32)
    )
    hidden = hidden_in.astype(jnp.float32)
    pos_group = positions[0]
    id_group = seg_ids[0]
    own_start = seq_place * row_count
    pos_own = lax.dynamic_slice_in_dim(pos_group, own_start, row_count)
    id_own = lax.dynamic_slice_in_dim(id_group, own_start, row_count)
    angles = turn_angles(pos_own)
    normed_in, inverse_in = norm_forward(hidden)
    attn_in = (normed_in * gain_in).astype(jnp.bfloat16)
    projected = jnp.dot(attn_in, qkv_full, preferred_element_type=jnp.float32)
    query_raw = projected[:, : H * HD].reshape(row_count, H, HD)
    key_raw = projected[:, H * HD : (H + 1) * HD]
    value_low = projected[:, (H + 1) * HD :].astype(jnp.bfloat16)
    query_normed, query_inverse = norm_forward(query_raw)
    query_low = (rope_turn(query_normed * gain_query, angles[:, None, :]) * query_scale).astype(
        jnp.bfloat16
    )
    key_normed, key_inverse = norm_forward(key_raw)
    key_low = rope_turn(key_normed * gain_key, angles).astype(jnp.bfloat16)
    key_parts = []
    value_parts = []
    pos_parts = []
    id_parts = []
    live_parts = []
    back_step = 1
    got_key, got_value = from_behind((key_low, value_low), "seq", back_step)
    source = seq_place - back_step
    source_start = jnp.maximum(source, 0) * row_count
    key_parts.append(got_key)
    value_parts.append(got_value)
    pos_parts.append(lax.dynamic_slice_in_dim(pos_group, source_start, row_count))
    id_parts.append(lax.dynamic_slice_in_dim(id_group, source_start, row_count))
    live_parts.append(jnp.broadcast_to(source >= 0, (row_count,)))
    key_parts.append(key_low)
    value_parts.append(value_low)
    pos_parts.append(pos_own)
    id_parts.append(id_own)
    live_parts.append(jnp.ones((row_count,), dtype=bool))
    keys_all = jnp.concatenate(key_parts, 0)
    values_all = jnp.concatenate(value_parts, 0)
    pos_keys = jnp.concatenate(pos_parts, 0)
    id_keys = jnp.concatenate(id_parts, 0)
    live_keys = jnp.concatenate(live_parts, 0)
    pos_gap = pos_own[:, None] - pos_keys[None, :]
    allowed = (
        live_keys[None, :]
        & (id_own[:, None] == id_keys[None, :])
        & (pos_gap >= 0)
        & (pos_gap < WINDOW)
    )
    scores = jnp.einsum("qhd,kd->hqk", query_low, keys_all, preferred_element_type=jnp.float32)
    scores = jnp.where(allowed[None], scores, MASKED_OUT)
    top_score = jnp.max(scores, -1, keepdims=True)
    weights_exp = jnp.exp(scores - top_score)
    weight_sum = jnp.sum(weights_exp, -1, keepdims=True)
    log_total = top_score + jnp.log(weight_sum)
    probs_low = (weights_exp / weight_sum).astype(jnp.bfloat16)
    attended = jnp.einsum("hqk,kd->qhd", probs_low, values_all, preferred_element_type=jnp.float32)
    attended = attended.reshape(row_count, H * HD).astype(jnp.bfloat16)
    branch = jnp.dot(attended, out_full, preferred_element_type=jnp.float32)
    branch_normed, branch_inverse = norm_forward(branch)
    middle = hidden + branch_normed * gain_attn_post
    ffn_normed, ffn_inverse = norm_forward(middle)
    ffn_in = (ffn_normed * gain_ffn_pre).astype(jnp.bfloat16)
    gate_up = jnp.dot(ffn_in, gate_up_full, preferred_element_type=jnp.float32)
    mixed_val, gelu_pull = jax.vjp(
        lambda gate_in, up_in: jax.nn.gelu(gate_in, approximate=True) * up_in,
        gate_up[:, :FF],
        gate_up[:, FF:],
    )
    mixed = mixed_val.astype(jnp.bfloat16)
    down_val = jnp.dot(mixed, down_full, preferred_element_type=jnp.float32)
    down_normed, down_inverse = norm_forward(down_val)
    output = (middle + down_normed * gain_ffn_post).astype(jnp.bfloat16)
    back_parts, back_qkv, back_out = (
        lax.all_gather(norm_gains, ("dp", "seq"), axis=0, tiled=True),
        lax.all_gather(w_qkv, ("dp", "seq"), axis=1, tiled=True),
        lax.all_gather(w_out, ("dp", "seq"), axis=0, tiled=True),
    )
    back_gate_up, back_down = (
        lax.all_gather(w_gate_up, ("dp", "seq"), axis=1, tiled=True),
        lax.all_gather(w_down, ("dp", "seq"), axis=0, tiled=True),
    )
    back_in, back_attn_post, back_ffn_pre, back_ffn_post, back_query, back_key = split_gains(
        back_parts.astype(jnp.float32)
    )
    grad_output = cotangent.astype(jnp.float32)
    grad_ffn_post = jnp.sum(grad_output * down_normed, 0)
    grad_down = norm_back(down_normed, down_inverse, grad_output * back_ffn_post).astype(
        jnp.bfloat16
    )
    grad_down_w = jnp.einsum("rf,rd->fd", mixed, grad_down, preferred_element_type=jnp.float32)
    grad_mixed = jnp.einsum("rd,fd->rf", grad_down, back_down, preferred_element_type=jnp.float32)
    grad_gate, grad_up = gelu_pull(grad_mixed)
    grad_gate_up = jnp.concatenate([grad_gate, grad_up], 1).astype(jnp.bfloat16)
    grad_gate_up_w = jnp.einsum(
        "rd,rf->df", ffn_in, grad_gate_up, preferred_element_type=jnp.float32
    )
    grad_ffn_in = jnp.einsum(
        "rf,df->rd", grad_gate_up, back_gate_up, preferred_element_type=jnp.float32
    )
    gate_up_share, down_share = (
        lax.psum_scatter(grad_gate_up_w, ("dp", "seq"), scatter_dimension=1, tiled=True),
        lax.psum_scatter(grad_down_w, ("dp", "seq"), scatter_dimension=0, tiled=True),
    )
    grad_ffn_pre = jnp.sum(grad_ffn_in * ffn_normed, 0)
    grad_middle = grad_output + norm_back(ffn_normed, ffn_inverse, grad_ffn_in * back_ffn_pre)
    grad_attn_post = jnp.sum(grad_middle * branch_normed, 0)
    grad_branch = norm_back(branch_normed, branch_inverse, grad_middle * back_attn_post).astype(
        jnp.bfloat16
    )
    grad_out_w = jnp.einsum("ra,rd->ad", attended, grad_branch, preferred_element_type=jnp.float32)
    grad_attended = jnp.einsum(
        "rd,ad->ra", grad_branch, back_out, preferred_element_type=jnp.float32
    )
    grad_attended = grad_attended.astype(jnp.bfloat16).reshape(row_count, H, HD)
    scores_again = jnp.einsum(
        "qhd,kd->hqk", query_low, keys_all, preferred_element_type=jnp.float32
    )
    scores_again = jnp.where(allowed[None], scores_again, MASKED_OUT)
    probs = jnp.exp(scores_again - log_total)
    probs_again = probs.astype(jnp.bfloat16)
    grad_probs = jnp.einsum(
        "qhd,kd->hqk", grad_attended, values_all, preferred_element_type=jnp.float32
    )
    grad_values = jnp.einsum(
        "hqk,qhd->kd", probs_again, grad_attended, preferred_element_type=jnp.float32
    )
    inner_sum = jnp.sum(probs * grad_probs, -1, keepdims=True)
    grad_scores = (probs * (grad_probs - inner_sum)).astype(jnp.bfloat16)
    grad_query = jnp.einsum(
        "hqk,kd->qhd", grad_scores, keys_all, preferred_element_type=jnp.float32
    )
    grad_keys = jnp.einsum(
        "hqk,qhd->kd", grad_scores, query_low, preferred_element_type=jnp.float32
    )
    own_first = reach_count * row_count
    grad_key_own = grad_keys[own_first:]
    grad_value_own = grad_values[own_first:]
    back_step = 1
    first_row = (reach_count - back_step) * row_count
    got_grad_key, got_grad_value = from_behind(
        (
            grad_keys[first_row : first_row + row_count],
            grad_values[first_row : first_row + row_count],
        ),
        "seq",
        -back_step,
    )
    grad_key_own = grad_key_own + got_grad_key
    grad_value_own = grad_value_own + got_grad_value
    grad_key_turn = rope_back(grad_key_own, angles)
    grad_key_gain = jnp.sum(grad_key_turn * key_normed, 0)
    grad_key_raw = norm_back(key_normed, key_inverse, grad_key_turn * back_key).astype(jnp.bfloat16)
    grad_query_turn = rope_back(grad_query * query_scale, angles[:, None, :])
    grad_query_gain = jnp.sum(grad_query_turn * query_normed, (0, 1))
    grad_query_raw = norm_back(query_normed, query_inverse, grad_query_turn * back_query)
    grad_query_raw = grad_query_raw.reshape(row_count, H * HD).astype(jnp.bfloat16)
    grad_projected = jnp.concatenate(
        [grad_query_raw, grad_key_raw, grad_value_own.astype(jnp.bfloat16)], 1
    )
    grad_qkv_w = jnp.einsum(
        "rd,rc->dc", attn_in, grad_projected, preferred_element_type=jnp.float32
    )
    grad_attn_in = jnp.einsum(
        "rc,dc->rd", grad_projected, back_qkv, preferred_element_type=jnp.float32
    )
    grad_in_gain = jnp.sum(grad_attn_in * normed_in, 0)
    input_grad = grad_middle + norm_back(normed_in, inverse_in, grad_attn_in * back_in)
    grad_gains = jnp.concatenate(
        [grad_in_gain, grad_attn_post, grad_ffn_pre, grad_ffn_post, grad_query_gain, grad_key_gain]
    )
    gain_share, qkv_share, out_share = (
        lax.psum_scatter(grad_gains, ("dp", "seq"), scatter_dimension=0, tiled=True),
        lax.psum_scatter(grad_qkv_w, ("dp", "seq"), scatter_dimension=1, tiled=True),
        lax.psum_scatter(grad_out_w, ("dp", "seq"), scatter_dimension=0, tiled=True),
    )
    return (output, input_grad, gain_share, qkv_share, out_share, gate_up_share, down_share)


def solution(mesh):
    in_specs = (
        P(("dp", "seq"), None),
        P(("dp", "seq"), None),
        P("dp", None),
        P("dp", None),
        P(("dp", "seq")),
        P(None, ("dp", "seq")),
        P(("dp", "seq"), None),
        P(None, ("dp", "seq")),
        P(("dp", "seq"), None),
    )
    out_specs = (
        P(("dp", "seq"), None),
        P(("dp", "seq"), None),
        P(("dp", "seq")),
        P(None, ("dp", "seq")),
        P(("dp", "seq"), None),
        P(None, ("dp", "seq")),
        P(("dp", "seq"), None),
    )
    return jax.shard_map(body, mesh=mesh, in_specs=in_specs, out_specs=out_specs, check_vma=False)
```

profile of v0, /device:TPU:0, one launch (start us, length us, event | category | flops | bytes accessed | tf_op | source)
XLA Modules:
  0.0 843.6 jit_solution(9990656419532347007)
XLA Ops:
  10.9 42.1 %all-reduce.1 = bf16[3072]{0:T(1024)(128)(2,1)S(1)} all-reduce(bf16[3072]{0:T(1024)(128)(2,1)S(1)} %dynamic-update-slice), channel_id=1, replica_groups=mesh['dp'=8,'seq'=4] {'dp','seq'}, use_global_device_ids=true, to_apply=%add.1 | all-reduce | flops 3072 | bytes 12288
  58.6 11.3 %all-gather.5.cloned.1.call-done = bf16[640,1536]{0,1:T(8,128)(2,1)} async-done(((bf16[640,48]{0,1:T(8,128)(2,1)}), bf16[640,1536]{0,1:T(8,128)(2,1)}) %all-gather.5.cloned.1.call-update) | async-done | bytes 1966096 | tf_op jit(solution)/shard_map/all_gather | solution.py:87
  69.8 3.2 fusion.68
  76.9 2.2 multiply_reduce_fusion.2
  83.5 2.2 collective-permute-start.1
  85.7 3.2 collective-permute-start
  97.2 3.6 fusion.32
  100.8 25.1 %all-gather.7.cloned.1.call-done = bf16[1024,640]{1,0:T(8,128)(2,1)} async-done(((bf16[32,640]{1,0:T(8,128)(2,1)}), bf16[1024,640]{1,0:T(8,128)(2,1)}) %all-gather.7.cloned.1.call-update) | async-done | bytes 1310736 | tf_op jit(solution)/shard_map/all_gather | solution.py:88
  125.9 2.8 multiply_reduce_fusion.9
  130.9 69.1 %all-gather.9.cloned.1.call-done = bf16[640,4096]{1,0:T(8,128)(2,1)} async-done(((bf16[640,128]{1,0:T(8,128)(2,1)}), bf16[640,4096]{1,0:T(8,128)(2,1)}) %all-gather.9.cloned.1.call-update) | async-done | bytes 5242896 | tf_op jit(solution)/shard_map/all_gather | solution.py:91
  200.0 5.5 fusion.86
  205.5 3.3 copy-done.1
  208.7 2.5 multiply_convert_fusion.1
  211.2 47.7 %all-gather.11.cloned.1.call-done = bf16[2048,640]{1,0:T(8,128)(2,1)} async-done(((bf16[64,640]{1,0:T(8,128)(2,1)}), bf16[2048,640]{1,0:T(8,128)(2,1)}) %all-gather.11.cloned.1.call-update) | async-done | bytes 2621456 | tf_op jit(solution)/shard_map/all_gather | solution.py:92
  258.9 4.4 multiply_reduce_fusion.7
  265.8 5.0 fusion.14
  270.9 4.1 multiply_reduce_fusion.3
  278.2 2.5 fusion.89
  280.7 3.6 convolution_convert_fusion
  284.3 2.3 copy.128
  286.5 5.5 fusion.33
  295.3 6.6 fusion
  301.9 4.7 fusion.2
  326.2 3.4 fusion.47
  331.2 5.2 fusion.90
  338.0 8.6 %fusion.19 = f32[640,4096]{1,0:T(8,128)} fusion(bf16[512,2048]{1,0:T(8,128)(2,1)} %copy-done.26, bf16[512,2048]{1,0:T(8,128)(2,1)S(1)} %copy-done.25, f32[512,640]{1,0:T(8,128)S(1)} %get-tuple-element.19, f32[640]{0:T(1024)S(1)} %get-tuple-element.41, f32[512]{0:T(512)S(1)} %add_rsqrt_fusion.2), kind=kOutput, calls=%fused_computation.32 | convolution fusion | flops 2693726208 | bytes 15995392 | tf_op jit(solution)/shard_map/rd,rf->df/dot_general | solution.py:192
  347.8 4.1 fusion.44
  352.0 41.3 %all-reduce.2 = f32[3072]{0:T(1024)S(1)} all-reduce(f32[3072]{0:T(1024)S(1)} %constant_dynamic-update-slice_fusion), channel_id=2, replica_groups=mesh['dp'=8,'seq'=4] {'dp','seq'}, use_global_device_ids=true, to_apply=%region_22.23.clone | all-reduce | flops 3072 | bytes 24576
  396.7 36.9 %reduce-scatter.7.cloned.1.call-done = f32[32,640]{1,0:T(8,128)} async-done(((f32[1024,640]{1,0:T(8,128)}), f32[32,640]{1,0:T(8,128)}) %reduce-scatter.7.cloned.1.call-update) | async-done | bytes 81936 | tf_op jit(solution)/shard_map/reduce_scatter | solution.py:272
  433.6 105.9 %reduce-scatter.5.cloned.1.call-done = f32[640,48]{0,1:T(8,128)} async-done(((f32[640,1536]{0,1:T(8,128)}), f32[640,48]{0,1:T(8,128)}) %reduce-scatter.5.cloned.1.call-update) | async-done | bytes 122896 | tf_op jit(solution)/shard_map/reduce_scatter | solution.py:271
  539.5 145.3 %reduce-scatter.11.cloned.1.call-done = f32[64,640]{1,0:T(8,128)} async-done(((f32[2048,640]{1,0:T(8,128)}), f32[64,640]{1,0:T(8,128)}) %reduce-scatter.11.cloned.1.call-update) | async-done | bytes 163856 | tf_op jit(solution)/shard_map/reduce_scatter | solution.py:200
  684.8 151.7 %reduce-scatter.9.cloned.1.call-done = f32[640,128]{1,0:T(8,128)} async-done(((f32[640,4096]{1,0:T(8,128)}), f32[640,128]{1,0:T(8,128)}) %reduce-scatter.9.cloned.1.call-update) | async-done | bytes 327696 | tf_op jit(solution)/shard_map/reduce_scatter | solution.py:199
  (257 shorter events, 63.3 us)
Async XLA Ops:
  7.2 62.7 %all-gather.5.cloned.1.call-start = ((), (), s32[]{:S(2)}) async-start(), calls=%async_computation.4 | async-start | bytes 2027520 | tf_op jit(solution)/shard_map/all_gather | solution.py:87
  7.9 118.0 %all-gather.7.cloned.1.call-start = ((), (), s32[]{:S(2)}) async-start(), calls=%async_computation.5 | async-start | bytes 1351680 | tf_op jit(solution)/shard_map/all_gather | solution.py:88
  8.7 191.3 %all-gather.9.cloned.1.call-start = ((), (), s32[]{:S(2)}) async-start(), calls=%async_computation.6 | async-start | bytes 5406720 | tf_op jit(solution)/shard_map/all_gather | solution.py:91
  9.4 249.5 %all-gather.11.cloned.1.call-start = ((), (), s32[]{:S(2)}) async-start(), calls=%async_computation.7 | async-start | bytes 2703360 | tf_op jit(solution)/shard_map/all_gather | solution.py:92
  10.0 423.6 %reduce-scatter.7.cloned.1.call-start = ((), (), s32[]{:S(2)}) async-start(), calls=%async_computation.9 | async-start | bytes 2703360 | tf_op jit(solution)/shard_map/reduce_scatter | solution.py:272
  53.6 19.5 %copy-start.61 = (f32[640]{0:T(1024)}, f32[640]{0:T(1024)S(1)}, u32[]{:S(2)}) copy-start(f32[640]{0:T(1024)S(1)} %get-tuple-element.43) | copy-start | bytes 7684
  53.6 75.2 %copy-start.45 = (f32[640]{0:T(1024)}, f32[640]{0:T(1024)S(1)}, u32[]{:S(2)}) copy-start(f32[640]{0:T(1024)S(1)} %get-tuple-element.42) | copy-start | bytes 7684
  53.6 26.5 %copy-start.65 = (f32[256]{0:T(256)}, f32[256]{0:T(256)S(1)}, u32[]{:S(2)}) copy-start(f32[256]{0:T(256)S(1)} %get-tuple-element.44) | copy-start | bytes 3076
  53.6 26.9 %copy-start.63 = (f32[256]{0:T(256)}, f32[256]{0:T(256)S(1)}, u32[]{:S(2)}) copy-start(f32[256]{0:T(256)S(1)} %get-tuple-element.45) | copy-start | bytes 3076
  56.8 16.2 %copy-start.68 = (f32[512]{0:T(512)}, f32[512]{0:T(512)S(1)}, u32[]{:S(2)}) copy-start(f32[512]{0:T(512)S(1)} %add_rsqrt_fusion.5) | copy-start | bytes 6148
  58.6 36.2 %copy-start.10 = (pred[512,1024]{0,1:T(8,128)(4,1)}, pred[512,1024]{0,1:T(8,128)(4,1)S(1)}, u32[]{:S(2)}) copy-start(pred[512,1024]{0,1:T(8,128)(4,1)S(1)} %fusion.23) | copy-start | bytes 1572868
  74.8 19.9 %copy-start.27 = (bf16[512,256]{1,0:T(8,128)(2,1)}, bf16[512,256]{1,0:T(8,128)(2,1)S(1)}, u32[]{:S(2)}) copy-start(bf16[512,256]{1,0:T(8,128)(2,1)S(1)} %slice.168) | copy-start | bytes 786436
  80.4 8.5 %copy-start.30 = (f32[512,4]{1,0:T(8,128)S(1)}, f32[512,4]{1,0:T(8,128)}, u32[]{:S(2)}) copy-start(f32[512,4]{1,0:T(8,128)} %copy.127) | copy-start | bytes 24580
  83.4 7.9 copy-start.20
  83.4 7.9 copy-start.22
  83.5 8.2 copy-start.38
  83.5 8.1 collective-permute-start.1
  85.7 9.0 %collective-permute-start = (bf16[512,256]{1,0:T(8,128)(2,1)S(1)}, bf16[512,256]{1,0:T(8,128)(2,1)S(1)}, u32[]{:S(2)}, u32[]{:S(2)}) collective-permute-start(bf16[512,256]{1,0:T(8,128)(2,1)S(1)} %slice.168), channel_id=1, source_target_pairs={{0,1},{1,2},{2,3},{4,5},{5,6},{6,7},{8,9},{9,10},{10,11},{12,13},{... | collective-permute-start | bytes 786440 | tf_op jit(solution)/shard_map/ppermute | solution.py:20
  94.7 6.1 copy-start.54
  258.9 6.8 copy-start.2
  264.5 6.4 slice-start
  265.8 5.1 copy-start.18
  265.8 5.1 slice-start.1
  293.9 30.4 %collective-permute-start.3 = (f32[512,256]{1,0:T(8,128)}, f32[512,256]{1,0:T(8,128)}, u32[]{:S(2)}, u32[]{:S(2)}) collective-permute-start(f32[512,256]{1,0:T(8,128)} %slice.121), channel_id=1, source_target_pairs={{1,0},{2,1},{3,2},{5,4},{6,5},{7,6},{9,8},{10,9},{11,10},{13,12},{... | collective-permute-start | bytes 1572872 | tf_op jit(solution)/shard_map/ppermute | solution.py:20
  295.2 244.2 %reduce-scatter.5.cloned.1.call-start = ((), (), s32[]{:S(2)}) async-start(), calls=%async_computation.8 | async-start | bytes 4055040 | tf_op jit(solution)/shard_map/reduce_scatter | solution.py:271
  295.3 6.6 copy-start.11
  295.3 6.6 copy-start.44
  309.8 10.8 %collective-permute-start.2 = (f32[512,256]{1,0:T(8,128)}, f32[512,256]{1,0:T(8,128)}, u32[]{:S(2)}, u32[]{:S(2)}) collective-permute-start(f32[512,256]{1,0:T(8,128)} %slice.117), channel_id=1, source_target_pairs={{1,0},{2,1},{3,2},{5,4},{6,5},{7,6},{9,8},{10,9},{11,10},{13,12},{... | collective-permute-start | bytes 1572872 | tf_op jit(solution)/shard_map/ppermute | solution.py:20
  320.5 5.0 copy-start.37
  329.6 355.2 %reduce-scatter.11.cloned.1.call-start = ((), (), s32[]{:S(2)}) async-start(), calls=%async_computation.11 | async-start | bytes 5406720 | tf_op jit(solution)/shard_map/reduce_scatter | solution.py:200
  336.4 500.1 %reduce-scatter.9.cloned.1.call-start = ((), (), s32[]{:S(2)}) async-start(), calls=%async_computation.10 | async-start | bytes 10813440 | tf_op jit(solution)/shard_map/reduce_scatter | solution.py:199
  347.8 46.8 %copy-start.8 = (f32[512,640]{1,0:T(8,128)S(1)}, f32[512,640]{1,0:T(8,128)}, u32[]{:S(2)}) copy-start(f32[512,640]{1,0:T(8,128)} %copy-done.7) | copy-start | bytes 3932164
  (60 other events, 157.0 us)
Sparse Core Ops, SparseCore 0:
  10.9 58.8 all-gather.4
  72.7 53.1 all-gather.6
  128.8 71.1 all-gather.8
  202.7 56.1 all-gather.10
  295.4 138.1 reduce-scatter.6
  439.4 100.0 reduce-scatter.4
  542.3 142.4 reduce-scatter.10
  687.7 148.7 reduce-scatter.8
where the time goes:
time: 852 us; the launch traced here: 844 us
  waiting for transfers between devices  596 us (70%)
  blocking collectives  83.4 us (10%)
  matrix products  72.6 us (9%)
  local copies, waits for them, and re-layouts  34.7 us (4%)
  other arithmetic  32.8 us (4%)
  between operations  15.6 us (2%)
  starting transfers between devices  8.8 us (1%)
    reduce_scatter x1, waiting for transfers between devices, body(): lax.psum_scatter(grad_gate_up_w, ('dp', 'seq'), scatter_dimension=1, tile...  152 us
    reduce_scatter x1, waiting for transfers between devices, body(): lax.psum_scatter(grad_down_w, ('dp', 'seq'), scatter_dimension=0, tiled=T...  145 us
    reduce_scatter x1, waiting for transfers between devices, body(): lax.psum_scatter(grad_qkv_w, ('dp', 'seq'), scatter_dimension=1, tiled=True)  106 us
    unnamed x2, blocking collectives  83.4 us
    all_gather x1, waiting for transfers between devices, body(): lax.all_gather(w_gate_up, ('dp', 'seq'), axis=1, tiled=True)  69.1 us
    all_gather x1, waiting for transfers between devices, body(): lax.all_gather(w_down, ('dp', 'seq'), axis=0, tiled=True)  47.7 us
    reduce_scatter x1, waiting for transfers between devices, body(): lax.psum_scatter(grad_out_w, ('dp', 'seq'), scatter_dimension=0, tiled=True)  36.9 us
    all_gather x1, waiting for transfers between devices, body(): lax.all_gather(w_out, ('dp', 'seq'), axis=0, tiled=True)  25.1 us
  transfers between devices with their start and end apart: 12, of which 8 were waited for; matrix products, arithmetic and copies ran while one was open for 11% of the time, Pallas kernels for 0%

commit v1 on v0

--- a/solution.py
+++ b/solution.py
@@ -1,6 +1,8 @@
 import jax
 import jax.numpy as jnp
 from jax import lax
+from jax.experimental import pallas as pl
+from jax.experimental.pallas import tpu as pltpu
 from jax.sharding import PartitionSpec as P
 
 D = 640
@@ -76,21 +78,220 @@
     )
 
 
+def bit_orders():
+    dp_bits = lax.axis_size("dp").bit_length() - 1
+    seq_bits = lax.axis_size("seq").bit_length() - 1
+    places = [("dp", b) for b in reversed(range(dp_bits))]
+    places += [("seq", b) for b in reversed(range(seq_bits))]
+    far = [("dp", b) for b in reversed(range(1, dp_bits))]
+    low_dp = [("dp", 0)]
+    high_seq = [("seq", b) for b in reversed(range(1, seq_bits))]
+    last = [("seq", 0)]
+    return places, far, low_dp + high_seq, high_seq + low_dp, last
+
+
+def swap(block, axis, bit):
+    route = [(i, i ^ (1 << bit)) for i in range(lax.axis_size(axis))]
+    return lax.ppermute(block, axis, route)
+
+
+def own_bit(axis, bit):
+    return (lax.axis_index(axis) >> bit) & 1
+
+
+def cut_rows(rows):
+    tiles = rows // 16
+    count = min(6, tiles)
+    edges = [tiles * k // count * 16 for k in range(count + 1)]
+    return [(edges[k], edges[k + 1] - edges[k]) for k in range(count)]
+
+
+def gather_kernel(pack_ref, full_ref, local_sem, send_sem, recv_sem):
+    far_size, _, high_size = full_ref.shape[:3]
+    dp_at = lax.axis_index("dp")
+    seq_at = lax.axis_index("seq")
+    far, low = dp_at // 2, dp_at % 2
+    high, core = seq_at // 2, seq_at % 2
+    far_peers = [(((far + d) % far_size) * 2 + low, seq_at) for d in range(1, far_size)]
+    low_peer = [(far * 2 + 1 - low, seq_at)]
+    high_peers = [(dp_at, ((high + d) % high_size) * 2 + core) for d in range(1, high_size)]
+    core_peer = [(dp_at, high * 2 + 1 - core)]
+    groups = [far_peers, low_peer, high_peers, core_peer]
+    slots = [0, far_size - 1, far_size, far_size + high_size - 1]
+    barrier = pltpu.get_barrier_semaphore()
+    peers = far_peers + low_peer + high_peers + core_peer
+    for peer in peers:
+        pl.semaphore_signal(barrier, inc=1, device_id=peer, device_id_type=pl.DeviceIdType.MESH)
+    pl.semaphore_wait(barrier, len(peers))
+    chunks = cut_rows(pack_ref.shape[0])
+    every = slice(None)
+
+    def copies(chunk, stage):
+        start, size = chunks[chunk]
+        rows = pl.ds(start, size)
+        low_first = chunk % 2 == 0
+        if stage == 0:
+            kind, src, place = 0, pack_ref.at[rows], (far, low, high, core)
+        elif stage == 3:
+            kind, src, place = 3, None, (every, every, every, core)
+        elif stage == 1:
+            kind, src, place = (1 if low_first else 2), None, (every, low, high, core)
+        elif low_first:
+            kind, src, place = 2, None, (every, every, high, core)
+        else:
+            kind, src, place = 1, None, (every, low, every, core)
+        target = full_ref.at[place + (rows,)]
+        return [
+            pltpu.make_async_remote_copy(
+                src_ref=target if src is None else src,
+                dst_ref=target,
+                send_sem=send_sem.at[chunk, slots[kind] + k],
+                recv_sem=recv_sem.at[chunk, slots[kind] + k],
+                device_id=peer,
+                device_id_type=pl.DeviceIdType.MESH,
+            )
+            for k, peer in enumerate(groups[kind])
+        ]
+
+    for chunk in range(len(chunks)):
+        for copy in copies(chunk, 0):
+            copy.start()
+    own = pltpu.make_async_copy(pack_ref, full_ref.at[far, low, high, core], local_sem)
+    own.start()
+    own.wait()
+    for turn in range((len(chunks) + 1) // 2 + 3):
+        for stage in range(4):
+            for chunk in (2 * (turn - stage), 2 * (turn - stage) + 1):
+                if 0 <= chunk < len(chunks):
+                    for copy in copies(chunk, stage):
+                        copy.wait_recv()
+                    if stage < 3:
+                        for copy in copies(chunk, stage + 1):
+                            copy.start()
+    for chunk in range(len(chunks)):
+        for stage in range(4):
+            for copy in copies(chunk, stage):
+                copy.wait_send()
+
+
+def gather_rows(pack):
+    far_size = lax.axis_size("dp") // 2
+    high_size = lax.axis_size("seq") // 2
+    chunk_count = len(cut_rows(pack.shape[0]))
+    sem_count = far_size + high_size
+    full = pl.pallas_call(
+        gather_kernel,
+        out_shape=jax.ShapeDtypeStruct((far_size, 2, high_size, 2) + pack.shape, pack.dtype),
+        in_specs=[pl.BlockSpec(memory_space=pl.ANY)],
+        out_specs=pl.BlockSpec(memory_space=pl.ANY),
+        scratch_shapes=[
+            pltpu.SemaphoreType.DMA,
+            pltpu.SemaphoreType.DMA((chunk_count, sem_count)),
+            pltpu.SemaphoreType.DMA((chunk_count, sem_count)),
+        ],
+        compiler_params=pltpu.CompilerParams(collective_id=0, has_side_effects=True),
+    )(pack)
+    return full.reshape((-1,) + pack.shape)
+
+
+def pack_exact(values):
+    high = lax.reduce_precision(values, 8, 7)
+    row = jnp.concatenate([high, values - high], -1).astype(jnp.bfloat16)
+    pads = [(0, 0)] * (row.ndim - 1) + [(0, 15), (0, D - row.shape[-1])]
+    return jnp.pad(row[..., None, :], pads)
+
+
+def unpack_exact(rows, length):
+    row = rows[..., 0, : 2 * length].astype(jnp.float32)
+    return row[..., :length] + row[..., length:]
+
+
+def take_half(block, mine, at):
+    return (
+        lax.dynamic_index_in_dim(block, 1 - mine, at, keepdims=False),
+        lax.dynamic_index_in_dim(block, mine, at, keepdims=False),
+    )
+
+
+def scatter_steps(block, exact, steps, left, places, final=False):
+    left = list(left)
+    for number, (axis, bit) in enumerate(reversed(steps)):
+        at = left.index((axis, bit))
+        mine = own_bit(axis, bit)
+        give, keep = take_half(block, mine, at)
+        rows = give.shape[-2]
+        if exact is not None:
+            exact_give, exact_keep = take_half(exact, mine, at)
+            give = jnp.concatenate([give, pack_exact(exact_give)], -2)
+        got = swap(give, axis, bit)
+        block = keep.astype(jnp.float32) + got[..., :rows, :].astype(jnp.float32)
+        if not (final and number == len(steps) - 1):
+            block = block.astype(jnp.bfloat16)
+        if exact is not None:
+            exact = exact_keep + unpack_exact(got[..., rows:, :], exact.shape[-1])
+        left.remove((axis, bit))
+    return block, exact
+
+
+def scatter_last(first, second, exact, plan):
+    places, far, order_a, order_b, last = plan
+    bits = (2,) * len(places)
+    first = first.reshape(bits + first.shape[-2:])
+    second = second.reshape(bits + second.shape[-2:])
+    if exact is not None:
+        exact = exact.reshape(bits + (-1,))
+    first, _ = scatter_steps(first, None, last, places, places)
+    second, exact = scatter_steps(second, exact, last, places, places)
+    return first, second, exact
+
+
+def scatter_near(first, second, exact, plan):
+    places, far, order_a, order_b, last = plan
+    left = far + [p for p in places if p not in far and p not in last]
+    first, _ = scatter_steps(first, None, order_a, left, places)
+    second, exact = scatter_steps(second, exact, order_b, left, places)
+    return jnp.concatenate([first, second], -2), exact
+
+
+def scatter_far(both, exact, plan):
+    places, far, order_a, order_b, last = plan
+    return scatter_steps(both, exact, far, far, places, final=True)
+
+
 def body(hidden_in, cotangent, seg_ids, positions, norm_gains, w_qkv, w_out, w_gate_up, w_down):
     row_count = hidden_in.shape[0]
     seq_count = lax.axis_size("seq")
     seq_place = lax.axis_index("seq")
     reach_count = min(seq_count - 1, (WINDOW + row_count - 2) // row_count)
     query_scale = HD ** (-0.5)
-    gain_parts, qkv_full, out_full = (
-        lax.all_gather(norm_gains, ("dp", "seq"), axis=0, tiled=True),
-        lax.all_gather(w_qkv, ("dp", "seq"), axis=1, tiled=True),
-        lax.all_gather(w_out, ("dp", "seq"), axis=0, tiled=True),
-    )
-    gate_up_full, down_full = (
-        lax.all_gather(w_gate_up, ("dp", "seq"), axis=1, tiled=True),
-        lax.all_gather(w_down, ("dp", "seq"), axis=0, tiled=True),
-    )
+    plan = bit_orders()
+    device_count = lax.axis_size("dp") * seq_count
+    gain_len = norm_gains.shape[0]
+    qkv_rows = w_qkv.shape[1]
+    out_rows = w_out.shape[0]
+    gate_up_rows = w_gate_up.shape[1]
+    gain_row = jnp.pad(norm_gains.reshape(1, gain_len), ((0, 0), (0, D - gain_len)))
+    lead_rows = qkv_rows + out_rows
+    lead_pad = -(lead_rows + 1) % 16
+    ffn_start = lead_rows + 1 + lead_pad
+    pack = jnp.concatenate(
+        [
+            w_qkv.T,
+            w_out,
+            jnp.pad(gain_row, ((0, lead_pad), (0, 0))),
+            w_gate_up.T,
+            w_down,
+        ],
+        0,
+    )
+    pack = jnp.pad(pack, ((0, -pack.shape[0] % 16), (0, 0)))
+    full = gather_rows(pack)
+    qkv_full = full[:, :qkv_rows].reshape(-1, D)
+    out_full = full[:, qkv_rows:lead_rows].reshape(-1, D)
+    gain_parts = full[:, lead_rows, :gain_len].reshape(-1)
+    down_start = ffn_start + gate_up_rows
+    gate_up_full = full[:, ffn_start:down_start].reshape(-1, D)
+    down_full = full[:, down_start : down_start + w_down.shape[0]].reshape(-1, D)
     gain_in, gain_attn_post, gain_ffn_pre, gain_ffn_post, gain_query, gain_key = split_gains(
         gain_parts.astype(jnp.float32)
     )
@@ -103,7 +304,9 @@
     angles = turn_angles(pos_own)
     normed_in, inverse_in = norm_forward(hidden)
     attn_in = (normed_in * gain_in).astype(jnp.bfloat16)
-    projected = jnp.dot(attn_in, qkv_full, preferred_element_type=jnp.float32)
+    projected = jnp.einsum(
+        "rd,cd->rc", attn_in, qkv_full, preferred_element_type=jnp.float32
+    )
     query_raw = projected[:, : H * HD].reshape(row_count, H, HD)
     key_raw = projected[:, H * HD : (H + 1) * HD]
     value_low = projected[:, (H + 1) * HD :].astype(jnp.bfloat16)
@@ -119,7 +322,8 @@
     id_parts = []
     live_parts = []
     back_step = 1
-    got_key, got_value = from_behind((key_low, value_low), "seq", back_step)
+    got_pair = from_behind(jnp.concatenate([key_low, value_low], 1), "seq", back_step)
+    got_key, got_value = got_pair[:, :HD], got_pair[:, HD:]
     source = seq_place - back_step
     source_start = jnp.maximum(source, 0) * row_count
     key_parts.append(got_key)
@@ -158,7 +362,7 @@
     middle = hidden + branch_normed * gain_attn_post
     ffn_normed, ffn_inverse = norm_forward(middle)
     ffn_in = (ffn_normed * gain_ffn_pre).astype(jnp.bfloat16)
-    gate_up = jnp.dot(ffn_in, gate_up_full, preferred_element_type=jnp.float32)
+    gate_up = jnp.einsum("rd,fd->rf", ffn_in, gate_up_full, preferred_element_type=jnp.float32)
     mixed_val, gelu_pull = jax.vjp(
         lambda gate_in, up_in: jax.nn.gelu(gate_in, approximate=True) * up_in,
         gate_up[:, :FF],
@@ -168,46 +372,40 @@
     down_val = jnp.dot(mixed, down_full, preferred_element_type=jnp.float32)
     down_normed, down_inverse = norm_forward(down_val)
     output = (middle + down_normed * gain_ffn_post).astype(jnp.bfloat16)
-    back_parts, back_qkv, back_out = (
-        lax.all_gather(norm_gains, ("dp", "seq"), axis=0, tiled=True),
-        lax.all_gather(w_qkv, ("dp", "seq"), axis=1, tiled=True),
-        lax.all_gather(w_out, ("dp", "seq"), axis=0, tiled=True),
-    )
-    back_gate_up, back_down = (
-        lax.all_gather(w_gate_up, ("dp", "seq"), axis=1, tiled=True),
-        lax.all_gather(w_down, ("dp", "seq"), axis=0, tiled=True),
-    )
-    back_in, back_attn_post, back_ffn_pre, back_ffn_post, back_query, back_key = split_gains(
-        back_parts.astype(jnp.float32)
-    )
     grad_output = cotangent.astype(jnp.float32)
     grad_ffn_post = jnp.sum(grad_output * down_normed, 0)
-    grad_down = norm_back(down_normed, down_inverse, grad_output * back_ffn_post).astype(
+    grad_down = norm_back(down_normed, down_inverse, grad_output * gain_ffn_post).astype(
         jnp.bfloat16
     )
+    grad_mixed = jnp.einsum("rd,fd->rf", grad_down, down_full, preferred_element_type=jnp.float32)
     grad_down_w = jnp.einsum("rf,rd->fd", mixed, grad_down, preferred_element_type=jnp.float32)
-    grad_mixed = jnp.einsum("rd,fd->rf", grad_down, back_down, preferred_element_type=jnp.float32)
+    grad_down_w = grad_down_w.astype(jnp.bfloat16).reshape(device_count, -1, D)
     grad_gate, grad_up = gelu_pull(grad_mixed)
     grad_gate_up = jnp.concatenate([grad_gate, grad_up], 1).astype(jnp.bfloat16)
     grad_gate_up_w = jnp.einsum(
-        "rd,rf->df", ffn_in, grad_gate_up, preferred_element_type=jnp.float32
-    )
-    grad_ffn_in = jnp.einsum(
-        "rf,df->rd", grad_gate_up, back_gate_up, preferred_element_type=jnp.float32
-    )
-    gate_up_share, down_share = (
-        lax.psum_scatter(grad_gate_up_w, ("dp", "seq"), scatter_dimension=1, tiled=True),
-        lax.psum_scatter(grad_down_w, ("dp", "seq"), scatter_dimension=0, tiled=True),
+        "rf,rd->fd", grad_gate_up, ffn_in, preferred_element_type=jnp.float32
+    )
+    grad_gate_up_w = grad_gate_up_w.astype(jnp.bfloat16).reshape(device_count, -1, D)
+    grad_ffn_in = jnp.dot(grad_gate_up, gate_up_full, preferred_element_type=jnp.float32)
+    grad_down_w, grad_gate_up_w, grad_ffn_in = lax.optimization_barrier(
+        (grad_down_w, grad_gate_up_w, grad_ffn_in)
+    )
+    cut = (grad_down_w.shape[1] + gate_up_rows) // 2
+    ffn_a, ffn_b, _ = scatter_last(
+        grad_gate_up_w[:, :cut],
+        jnp.concatenate([grad_gate_up_w[:, cut:], grad_down_w], 1),
+        None,
+        plan,
     )
     grad_ffn_pre = jnp.sum(grad_ffn_in * ffn_normed, 0)
-    grad_middle = grad_output + norm_back(ffn_normed, ffn_inverse, grad_ffn_in * back_ffn_pre)
+    grad_middle = grad_output + norm_back(ffn_normed, ffn_inverse, grad_ffn_in * gain_ffn_pre)
     grad_attn_post = jnp.sum(grad_middle * branch_normed, 0)
-    grad_branch = norm_back(branch_normed, branch_inverse, grad_middle * back_attn_post).astype(
+    grad_branch = norm_back(branch_normed, branch_inverse, grad_middle * gain_attn_post).astype(
         jnp.bfloat16
     )
     grad_out_w = jnp.einsum("ra,rd->ad", attended, grad_branch, preferred_element_type=jnp.float32)
     grad_attended = jnp.einsum(
-        "rd,ad->ra", grad_branch, back_out, preferred_element_type=jnp.float32
+        "rd,ad->ra", grad_branch, out_full, preferred_element_type=jnp.float32
     )
     grad_attended = grad_attended.astype(jnp.bfloat16).reshape(row_count, H, HD)
     scores_again = jnp.einsum(
@@ -224,53 +422,68 @@
     )
     inner_sum = jnp.sum(probs * grad_probs, -1, keepdims=True)
     grad_scores = (probs * (grad_probs - inner_sum)).astype(jnp.bfloat16)
+    grad_scores, ffn_a, ffn_b = lax.optimization_barrier((grad_scores, ffn_a, ffn_b))
+    ffn_near, _ = scatter_near(ffn_a, ffn_b, None, plan)
     grad_query = jnp.einsum(
         "hqk,kd->qhd", grad_scores, keys_all, preferred_element_type=jnp.float32
     )
     grad_keys = jnp.einsum(
         "hqk,qhd->kd", grad_scores, query_low, preferred_element_type=jnp.float32
     )
+    grad_query, grad_keys, ffn_near = lax.optimization_barrier((grad_query, grad_keys, ffn_near))
+    ffn_share, _ = scatter_far(ffn_near, None, plan)
     own_first = reach_count * row_count
     grad_key_own = grad_keys[own_first:]
     grad_value_own = grad_values[own_first:]
     back_step = 1
     first_row = (reach_count - back_step) * row_count
-    got_grad_key, got_grad_value = from_behind(
-        (
-            grad_keys[first_row : first_row + row_count],
-            grad_values[first_row : first_row + row_count],
-        ),
+    got_grad = from_behind(
+        jnp.concatenate(
+            [
+                grad_keys[first_row : first_row + row_count],
+                grad_values[first_row : first_row + row_count],
+            ],
+            1,
+        ).astype(jnp.bfloat16),
         "seq",
         -back_step,
-    )
+    ).astype(jnp.float32)
+    got_grad_key, got_grad_value = got_grad[:, :HD], got_grad[:, HD:]
     grad_key_own = grad_key_own + got_grad_key
     grad_value_own = grad_value_own + got_grad_value
     grad_key_turn = rope_back(grad_key_own, angles)
     grad_key_gain = jnp.sum(grad_key_turn * key_normed, 0)
-    grad_key_raw = norm_back(key_normed, key_inverse, grad_key_turn * back_key).astype(jnp.bfloat16)
+    grad_key_raw = norm_back(key_normed, key_inverse, grad_key_turn * gain_key).astype(jnp.bfloat16)
     grad_query_turn = rope_back(grad_query * query_scale, angles[:, None, :])
     grad_query_gain = jnp.sum(grad_query_turn * query_normed, (0, 1))
-    grad_query_raw = norm_back(query_normed, query_inverse, grad_query_turn * back_query)
+    grad_query_raw = norm_back(query_normed, query_inverse, grad_query_turn * gain_query)
     grad_query_raw = grad_query_raw.reshape(row_count, H * HD).astype(jnp.bfloat16)
     grad_projected = jnp.concatenate(
         [grad_query_raw, grad_key_raw, grad_value_own.astype(jnp.bfloat16)], 1
     )
+    grad_projected, ffn_share = (grad_projected, ffn_share)
+    gate_up_share = ffn_share[:gate_up_rows].T
+    down_share = ffn_share[gate_up_rows:]
     grad_qkv_w = jnp.einsum(
-        "rd,rc->dc", attn_in, grad_projected, preferred_element_type=jnp.float32
+        "rc,rd->cd", grad_projected, attn_in, preferred_element_type=jnp.float32
     )
     grad_attn_in = jnp.einsum(
-        "rc,dc->rd", grad_projected, back_qkv, preferred_element_type=jnp.float32
+        "rc,cd->rd", grad_projected, qkv_full, preferred_element_type=jnp.float32
     )
     grad_in_gain = jnp.sum(grad_attn_in * normed_in, 0)
-    input_grad = grad_middle + norm_back(normed_in, inverse_in, grad_attn_in * back_in)
+    input_grad = grad_middle + norm_back(normed_in, inverse_in, grad_attn_in * gain_in)
     grad_gains = jnp.concatenate(
         [grad_in_gain, grad_attn_post, grad_ffn_pre, grad_ffn_post, grad_query_gain, grad_key_gain]
     )
-    gain_share, qkv_share, out_share = (
-        lax.psum_scatter(grad_gains, ("dp", "seq"), scatter_dimension=0, tiled=True),
-        lax.psum_scatter(grad_qkv_w, ("dp", "seq"), scatter_dimension=1, tiled=True),
-        lax.psum_scatter(grad_out_w, ("dp", "seq"), scatter_dimension=0, tiled=True),
-    )
+    parts = scatter_last(
+        grad_qkv_w.astype(jnp.bfloat16).reshape(device_count, -1, D),
+        grad_out_w.astype(jnp.bfloat16).reshape(device_count, -1, D),
+        grad_gains,
+        plan,
+    )
+    first_share, gain_share = scatter_far(*scatter_near(*parts, plan), plan)
+    qkv_share = first_share[:qkv_rows].T
+    out_share = first_share[qkv_rows:]
     return (output, input_grad, gain_share, qkv_share, out_share, gate_up_share, down_share)
 
 

time: 852 us -> 317 us (0.37)
  waiting for transfers between devices: 596 us -> 47.9 us
  blocking collectives: 83.4 us -> 0 us
  Pallas kernels: 0 us -> 79.6 us
  local copies, waits for them, and re-layouts: 34.7 us -> 56.4 us
  matrix products: 72.6 us -> 56.8 us
  other arithmetic: 32.8 us -> 46.5 us
  starting transfers between devices: 8.8 us -> 22.4 us
  between operations: 15.6 us -> 2.35 us
    reduce_scatter x4 -> x0, waiting for transfers between devices: 440 us -> none  [the longest x1 152 us: body(): lax.psum_scatter(grad_gate_up_w, ('dp', 'seq'), scatter_dimension=1, tile...]
    all_gather x4 -> x0, waiting for transfers between devices: 153 us -> none  [the longest x1 69.1 us: body(): lax.all_gather(w_gate_up, ('dp', 'seq'), axis=1, tiled=True)]
    unnamed x2 -> x0, blocking collectives: 83.4 us -> none
    pallas_call x0 -> x1, Pallas kernels: none -> 79.6 us  [gather_rows(): pl.pallas_call(gather_kernel, out_shape=jax.ShapeDtypeStruct((far_size, 2...]
    ppermute x0 -> x16, waiting for transfers between devices: none -> 47.9 us  [swap(): return lax.ppermute(block, axis, route)]
    dot_general x9 -> x8, matrix products: 44 us -> 24.8 us  [the longest x1 4.76 us: body(): jnp.einsum('rf,rd->fd', grad_gate_up, ffn_in, preferred_element_type=jnp....]
    ppermute x0 -> x16, starting transfers between devices: none -> 18 us  [swap(): return lax.ppermute(block, axis, route)]
    slice x0 -> x10, local copies, waits for them, and re-layouts: none -> 17 us  [the longest x1 5.72 us: body(): gate_up_full = full[:, ffn_start:down_start].reshape(-1, D)]
  transfers between devices with their start and end apart: 12 -> 18, of which waited for: 8 -> 9; matrix products, arithmetic and copies ran while one was open for 11% -> 29% of each run, Pallas kernels for 0% -> 0%
where the time goes in v1:
time: 317 us; the launch traced here: 312 us
  Pallas kernels  79.6 us (25%)
  matrix products  56.8 us (18%)
  local copies, waits for them, and re-layouts  56.4 us (18%)
  waiting for transfers between devices  47.9 us (15%)
  other arithmetic  46.5 us (15%)
  starting transfers between devices  22.4 us (7%)
    pallas_call x1, Pallas kernels, gather_rows(): pl.pallas_call(gather_kernel, out_shape=jax.ShapeDtypeStruct((far_size, 2...  79.6 us
    ppermute x16, waiting for transfers between devices, swap(): return lax.ppermute(block, axis, route)  47.9 us
    ppermute x16, starting transfers between devices, swap(): return lax.ppermute(block, axis, route)  18 us
    unnamed x171, local copies, waits for them, and re-layouts  15.1 us
    sub x1, matrix products, body(): grad_scores = (probs * (grad_probs - inner_sum)).astype(jnp.bfloat16)  12.8 us
    convert_element_type x14, other arithmetic, scatter_steps(): block = block.astype(jnp.bfloat16)  8.65 us
  transfers between devices with their start and end apart: 18, of which 9 were waited for; matrix products, arithmetic and copies ran while one was open for 29% of the time, Pallas kernels for 0%

profile of v1, /device:TPU:0, one launch (start us, length us, event | category | flops | bytes accessed | tf_op | source)
XLA Modules:
  0.0 312.0 jit_solution(623775155161175433)
XLA Ops:
  6.2 79.6 %shard_map.144 = bf16[4,2,2,2,288,640]{5,4,3,2,1,0:T(8,128)(2,1)} custom-call(bf16[288,640]{1,0:T(8,128)(2,1)} %copy-done.40), custom_call_target="tpu_custom_call" | custom-call | tf_op jit(solution)/shard_map/pallas_call | solution.py:182
  94.5 2.5 multiply_cosine_fusion
  97.8 3.1 %collective-permute-start = (bf16[512,512]{1,0:T(8,128)(2,1)}, bf16[512,512]{1,0:T(8,128)(2,1)}, u32[]{:S(2)}, u32[]{:S(2)}) collective-permute-start(bf16[512,512]{1,0:T(8,128)(2,1)} %pad_maximum_fusion.10), channel_id=1, source_target_pairs={{0,1},{1,2},{2,3},{4,5},{5,6},{6,7},{8,9},{9,10},{10,11},{12,13},{... | collective-permute-start | bytes 1572872 | tf_op jit(solution)/shard_map/ppermute | solution.py:22
  101.0 2.5 slice.261
  103.5 3.5 %slice.267 = bf16[32,64,640]{2,1,0:T(8,128)(2,1)} slice(bf16[32,288,640]{2,1,0:T(8,128)(2,1)} %bitcast.258), slice={[0:32], [224:288], [0:640]} | slice | bytes 5242880 | tf_op jit(solution)/shard_map/slice | solution.py:294
  107.0 5.7 %slice.264 = bf16[32,128,640]{2,1,0:T(8,128)(2,1)} slice(bf16[32,288,640]{2,1,0:T(8,128)(2,1)} %bitcast.259), slice={[0:32], [96:224], [0:640]} | slice | bytes 10485760 | tf_op jit(solution)/shard_map/slice | solution.py:293
  114.0 2.5 reshape.472
  116.5 2.2 multiply_reduce_fusion.2
  131.3 2.1 copy-done.6
  133.4 2.7 fusion.37
  138.0 3.5 %fusion.155 = f32[512,4096]{1,0:T(8,128)S(1)} fusion(bf16[4096,640]{1,0:T(8,128)(2,1)S(1)} %bitcast.272, f32[512,640]{1,0:T(8,128)S(1)} %get-tuple-element.100, f32[640]{0:T(1024)S(1)} %get-tuple-element.130, f32[512]{0:T(512)S(1)} %add_rsqrt_fusion.2), kind=kOutput, calls=%fused_computation.342 | convolution fusion | flops 2685337600 | bytes 14946816 | tf_op jit(solution)/shard_map/rd,fd->rf/dot_general | solution.py:365
  147.6 4.6 %fusion.14 = (bf16[512,2048]{1,0:T(8,128)(2,1)S(1)}, bf16[512,2048]{1,0:T(8,128)(2,1)S(1)}) fusion(f32[512,4096]{1,0:T(8,128)S(1)} %fusion.155, bf16[512,640]{1,0:T(8,128)(2,1)S(1)} %get-tuple-element.115, bf16[2048,640]{1,0:T(8,128)(2,1)S(1)} %bitcast.277), kind=kOutput, calls=%fused_computation.22 | convolution fusion | flops 1367343104 | bytes 15859712 | tf_op jit(solution)/shard_map/rd,fd->rf/dot_general | solution.py:380
  154.1 3.5 %fusion.21 = f32[512,640]{1,0:T(8,128)S(1)} fusion(bf16[4096,640]{1,0:T(8,128)(2,1)S(1)} %bitcast.273, bf16[512,2048]{1,0:T(8,128)(2,1)S(1)} %get-tuple-element.102, bf16[512,2048]{1,0:T(8,128)(2,1)S(1)} %get-tuple-element.101), kind=kOutput, calls=%fused_computation.40 | convolution fusion | flops 2692743168 | bytes 10747904 | tf_op jit(solution)/shard_map/dot_general | solution.py:389
  157.5 4.8 %convolution_convert_fusion = bf16[4096,640]{1,0:T(8,128)(2,1)S(1)} fusion(bf16[512,2048]{1,0:T(8,128)(2,1)S(1)} %get-tuple-element.102, bf16[512,2048]{1,0:T(8,128)(2,1)S(1)} %get-tuple-element.101, f32[512,640]{1,0:T(8,128)S(1)} %get-tuple-element.100, f32[640]{0:T(1024)S(1)} %get-tuple-element.130, f32[512]{0:T(512)S(1)} %add_rsqrt_fusion.2), kind=kOutput, calls=%fused_computation.11 | convolution fusion | flops 2696347648 | bytes 10752512 | tf_op jit(solution)/shard_map/rf,rd->fd/dot_general | solution.py:385
  169.8 2.3 constant_dynamic-slice_fusion.16
  172.1 2.3 copy.302
  174.4 3.2 %copy.337 = bf16[2,2,2,2,1,96,640]{6,5,1,0,3,2,4:T(8,128)(2,1)} copy(bf16[2,2,2,2,1,96,640]{6,5,4,3,2,1,0:T(8,128)(2,1)} %get-tuple-element.106) | data formatting | bytes 3932160 | tf_op jit(solution)/shard_map/jit(dynamic_index_in_dim)/dynamic_slice | solution.py:211
  178.1 6.1 %fusion.38 = f32[1024,256]{1,0:T(8,128)} fusion(bf16[512,4,256]{0,2,1:T(8,128)(2,1)S(1)} %bitcast.288, f32[1024,512,4]{1,0,2:T(8,128)} %copy-done.6, f32[4,512]{1,0:T(4,128)S(1)} %copy-done.66, pred[512,1024]{0,1:T(8,128)(4,1)S(1)} %fusion.24), kind=kOutput, calls=%fused_computation.80 | convolution fusion | flops 1080033280 | bytes 11018240 | tf_op jit(solution)/shard_map/hqk,qhd->kd/dot_general | solution.py:420
  184.2 12.8 %fusion.2 = bf16[4,512,1024]{1,2,0:T(8,128)(2,1)} fusion(f32[1024,512,4]{1,0,2:T(8,128)} %copy-done.6, f32[4,512]{1,0:T(4,128)S(1)} %copy-done.66, pred[512,1024]{0,1:T(8,128)(4,1)S(1)} %fusion.24, bf16[512,4,256]{0,2,1:T(8,128)(2,1)} %bitcast.287, bf16[512,256]{1,0:T(8,128)(2,1)S(1)} %copy-done.27, bf16[512,256]{1,0:T(8,128)(2,1)} %copy-done.43), kind=kOutput, calls=%fused_computation.4 | convolution fusion | flops 2166361088 | bytes 14688256 | tf_op jit(solution)/shard_map/sub | solution.py:424
  197.0 2.8 fusion.20
  202.0 2.4 collective-permute-start.5
  209.9 16.4 %collective-permute-done.5 = bf16[2,2,2,96,640]{4,3,1,0,2:T(8,128)(2,1)S(1)} collective-permute-done((bf16[2,2,2,96,640]{4,3,1,0,2:T(8,128)(2,1)S(1)}, bf16[2,2,2,96,640]{4,3,1,0,2:T(8,128)(2,1)S(1)}, u32[]{:S(2)}, u32[]{:S(2)}) %collective-permute-start.5) | collective-permute-done | bytes 983072 | tf_op jit(solution)/shard_map/ppermute | solution.py:95
  230.8 8.6 %collective-permute-done.6 = bf16[2,2,96,640]{3,2,1,0:T(8,128)(2,1)S(1)} collective-permute-done((bf16[2,2,96,640]{3,2,1,0:T(8,128)(2,1)S(1)}, bf16[2,2,96,640]{3,2,1,0:T(8,128)(2,1)S(1)}, u32[]{:S(2)}, u32[]{:S(2)}) %collective-permute-start.6) | collective-permute-done | bytes 491552 | tf_op jit(solution)/shard_map/ppermute | solution.py:95
  251.4 3.6 %multiply_reduce_fusion = (f32[1024]{0:T(1024)S(1)}, bf16[512,1024]{1,0:T(8,128)(2,1)}) fusion(f32[512,1024]{1,0:T(8,128)} %bitcast.268, f32[512,1024]{1,0:T(8,128)S(1)} %bitcast.267, f32[512,1536]{1,0:T(8,128)S(1)} %copy-done.3, f32[512,1024]{1,0:T(8,128)S(1)} %bitcast.269, f32[1024]{0:T(1024)S(1)} %bitcast.297), kind=kLoop, calls=%fused_computation.45 | loop fusion | flops 4193280 | bytes 9445376 | tf_op jit(solution)/shard_map/reduce_sum | solution.py:458
  259.8 2.5 fusion.49
  267.2 2.5 convolution_convert_fusion.2
  275.3 2.6 collective-permute-start.12
  277.9 9.1 %collective-permute-done.9 = bf16[2,2,2,48,640]{4,2,1,0,3:T(2,128)(2,1)S(1)} collective-permute-done((bf16[2,2,2,48,640]{4,2,1,0,3:T(2,128)(2,1)S(1)}, bf16[2,2,2,48,640]{4,2,1,0,3:T(2,128)(2,1)S(1)}, u32[]{:S(2)}, u32[]{:S(2)}) %collective-permute-start.9) | collective-permute-done | bytes 491552 | tf_op jit(solution)/shard_map/ppermute | solution.py:95
  291.3 3.3 %collective-permute-done.10 = bf16[2,2,48,640]{3,2,1,0:T(8,128)(2,1)S(1)} collective-permute-done((bf16[2,2,48,640]{3,2,1,0:T(8,128)(2,1)S(1)}, bf16[2,2,48,640]{3,2,1,0:T(8,128)(2,1)S(1)}, u32[]{:S(2)}, u32[]{:S(2)}) %collective-permute-start.10) | collective-permute-done | bytes 245792 | tf_op jit(solution)/shard_map/ppermute | solution.py:95
  299.0 3.7 %collective-permute-done.14 = bf16[2,96,640]{2,1,0:T(8,128)(2,1)S(1)} collective-permute-done((bf16[2,96,640]{2,1,0:T(8,128)(2,1)S(1)}, bf16[2,96,640]{2,1,0:T(8,128)(2,1)S(1)}, u32[]{:S(2)}, u32[]{:S(2)}) %collective-permute-start.14) | collective-permute-done | bytes 245792 | tf_op jit(solution)/shard_map/ppermute | solution.py:95
  303.0 2.6 collective-permute-start.15
  306.5 3.4 %collective-permute-done.15 = bf16[96,640]{1,0:T(8,128)(2,1)S(1)} collective-permute-done((bf16[96,640]{1,0:T(8,128)(2,1)S(1)}, bf16[96,640]{1,0:T(8,128)(2,1)S(1)}, u32[]{:S(2)}, u32[]{:S(2)}) %collective-permute-start.15) | collective-permute-done | bytes 122912 | tf_op jit(solution)/shard_map/ppermute | solution.py:95
  (340 shorter events, 96.8 us)
Async XLA Ops:
  87.4 6.4 %copy-start.59 = (f32[256]{0:T(256)}, f32[256]{0:T(256)S(1)}, u32[]{:S(2)}) copy-start(f32[256]{0:T(256)S(1)} %get-tuple-element.134) | copy-start | bytes 3076
  91.5 6.3 %copy-start.1 = (f32[512,1536]{1,0:T(8,128)}, f32[512,1536]{1,0:T(8,128)S(1)}, u32[]{:S(2)}) copy-start(f32[512,1536]{1,0:T(8,128)S(1)} %fusion.94) | copy-start | bytes 9437188
  92.6 4.3 %copy-start.26 = (bf16[512,256]{1,0:T(8,128)(2,1)S(1)}, bf16[512,256]{1,0:T(8,128)(2,1)}, u32[]{:S(2)}) copy-start(bf16[512,256]{1,0:T(8,128)(2,1)} %slice.390) | copy-start | bytes 786436
  93.8 18.9 %copy-start.51 = (f32[512]{0:T(512)}, f32[512]{0:T(512)S(1)}, u32[]{:S(2)}) copy-start(f32[512]{0:T(512)S(1)} %convert_element_type.363) | copy-start | bytes 6148
  97.8 28.3 %collective-permute-start = (bf16[512,512]{1,0:T(8,128)(2,1)}, bf16[512,512]{1,0:T(8,128)(2,1)}, u32[]{:S(2)}, u32[]{:S(2)}) collective-permute-start(bf16[512,512]{1,0:T(8,128)(2,1)} %pad_maximum_fusion.10), channel_id=1, source_target_pairs={{0,1},{1,2},{2,3},{4,5},{5,6},{6,7},{8,9},{9,10},{10,11},{12,13},{... | collective-permute-start | bytes 1572872 | tf_op jit(solution)/shard_map/ppermute | solution.py:22
  107.0 5.7 %copy-start.2 = (f32[512,1536]{1,0:T(8,128)S(1)}, f32[512,1536]{1,0:T(8,128)}, u32[]{:S(2)}) copy-start(f32[512,1536]{1,0:T(8,128)} %copy-done.1) | copy-start | bytes 9437188
  129.2 8.8 %slice-start = ((s8[5242880]{0:T(1024)(128)(4,1)}), s8[4194304]{0:T(1024)(128)(4,1)S(1)}, s32[]{:S(2)}) async-start(s8[5242880]{0:T(1024)(128)(4,1)} %bitcast.270), calls=%async_computation | async-start | bytes 8388608
  133.4 4.6 %slice-start.1 = ((s8[5242880]{0:T(1024)(128)(4,1)}), s8[1048576]{0:T(1024)(128)(4,1)S(1)}, s32[]{:S(2)}) async-start(s8[5242880]{0:T(1024)(128)(4,1)} %bitcast.270), calls=%async_computation.1 | async-start | bytes 2097152
  162.8 5.1 %copy-start = (bf16[32,96,640]{2,1,0:T(8,128)(2,1)}, bf16[32,96,640]{2,1,0:T(8,128)(2,1)S(1)}, u32[]{:S(2)}) copy-start(bf16[32,96,640]{2,1,0:T(8,128)(2,1)S(1)} %slice.211) | copy-start | bytes 11796484
  169.4 27.6 %collective-permute-start.1 = (bf16[2,2,2,2,96,640]{5,4,3,2,1,0:T(8,128)(2,1)}, bf16[2,2,2,2,96,640]{5,4,3,2,1,0:T(8,128)(2,1)}, u32[]{:S(2)}, u32[]{:S(2)}) collective-permute-start(bf16[2,2,2,2,96,640]{5,4,3,2,1,0:T(8,128)(2,1)} %dynamic-slice_bitcast_fusion), channel_id=1, source_target_pairs={{0,1},{1,0},{2,3},{3,2},{4,5},{5,4},{6,7},{7,6},{8,9},{9,8},{10,11... | collective-permute-start | bytes 5898248 | tf_op jit(solution)/shard_map/ppermute | solution.py:95
  177.6 22.3 %collective-permute-start.2 = (bf16[2,2,2,2,96,640]{5,4,1,0,3,2:T(8,128)(2,1)}, bf16[2,2,2,2,96,640]{5,4,1,0,3,2:T(8,128)(2,1)}, u32[]{:S(2)}, u32[]{:S(2)}) collective-permute-start(bf16[2,2,2,2,96,640]{5,4,1,0,3,2:T(8,128)(2,1)} %bitcast.248), channel_id=1, source_target_pairs={{0,1},{1,0},{2,3},{3,2},{4,5},{5,4},{6,7},{7,6},{8,9},{9,8},{10,11... | collective-permute-start | bytes 5898248 | tf_op jit(solution)/shard_map/ppermute | solution.py:95
  202.0 24.3 %collective-permute-start.5 = (bf16[2,2,2,96,640]{4,3,1,0,2:T(8,128)(2,1)S(1)}, bf16[2,2,2,96,640]{4,3,1,0,2:T(8,128)(2,1)S(1)}, u32[]{:S(2)}, u32[]{:S(2)}) collective-permute-start(bf16[2,2,2,96,640]{4,3,1,0,2:T(8,128)(2,1)S(1)} %dynamic-slice_bitcast_fusion.1), channel_id=1, source_target_pairs={{0,4},{4,0},{8,12},{12,8},{16,20},{20,16},{24,28},{28,24},{1,5},{5... | collective-permute-start | bytes 2949128 | tf_op jit(solution)/shard_map/ppermute | solution.py:95
  204.5 23.4 %collective-permute-start.3 = (bf16[2,2,2,96,640]{4,3,2,1,0:T(8,128)(2,1)S(1)}, bf16[2,2,2,96,640]{4,3,2,1,0:T(8,128)(2,1)S(1)}, u32[]{:S(2)}, u32[]{:S(2)}) collective-permute-start(bf16[2,2,2,96,640]{4,3,2,1,0:T(8,128)(2,1)S(1)} %dynamic-slice_bitcast_fusion.2), channel_id=1, source_target_pairs={{0,2},{1,3},{2,0},{3,1},{4,6},{5,7},{6,4},{7,5},{8,10},{9,11},{10,... | collective-permute-start | bytes 2949128 | tf_op jit(solution)/shard_map/ppermute | solution.py:95
  209.9 32.1 %copy-start.36 = (f32[1024,256]{1,0:T(8,128)}, f32[1024,256]{1,0:T(8,128)S(1)}, u32[]{:S(2)}) copy-start(f32[1024,256]{1,0:T(8,128)S(1)} %convolution_bitcast_fusion.1) | copy-start | bytes 3145732
  226.7 12.7 %collective-permute-start.6 = (bf16[2,2,96,640]{3,2,1,0:T(8,128)(2,1)S(1)}, bf16[2,2,96,640]{3,2,1,0:T(8,128)(2,1)S(1)}, u32[]{:S(2)}, u32[]{:S(2)}) collective-permute-start(bf16[2,2,96,640]{3,2,1,0:T(8,128)(2,1)S(1)} %dynamic-slice_bitcast_fusion.5), channel_id=1, source_target_pairs={{0,2},{1,3},{2,0},{3,1},{4,6},{5,7},{6,4},{7,5},{8,10},{9,11},{10,... | collective-permute-start | bytes 1474568 | tf_op jit(solution)/shard_map/ppermute | solution.py:95
  228.3 12.0 %collective-permute-start.4 = (bf16[2,2,96,640]{3,2,1,0:T(8,128)(2,1)S(1)}, bf16[2,2,96,640]{3,2,1,0:T(8,128)(2,1)S(1)}, u32[]{:S(2)}, u32[]{:S(2)}) collective-permute-start(bf16[2,2,96,640]{3,2,1,0:T(8,128)(2,1)S(1)} %dynamic-slice_bitcast_fusion.6), channel_id=1, source_target_pairs={{0,4},{4,0},{8,12},{12,8},{16,20},{20,16},{24,28},{28,24},{1,5},{5... | collective-permute-start | bytes 1474568 | tf_op jit(solution)/shard_map/ppermute | solution.py:95
  242.9 12.2 %collective-permute-start.7 = (bf16[512,512]{1,0:T(8,128)(2,1)}, bf16[512,512]{1,0:T(8,128)(2,1)}, u32[]{:S(2)}, u32[]{:S(2)}) collective-permute-start(bf16[512,512]{1,0:T(8,128)(2,1)} %pad_maximum_fusion.11), channel_id=1, source_target_pairs={{1,0},{2,1},{3,2},{5,4},{6,5},{7,6},{9,8},{10,9},{11,10},{13,12},{... | collective-permute-start | bytes 1572872 | tf_op jit(solution)/shard_map/ppermute | solution.py:22
  246.8 17.8 %collective-permute-start.16 = (bf16[2,192,640]{2,1,0:T(8,128)(2,1)}, bf16[2,192,640]{2,1,0:T(8,128)(2,1)}, u32[]{:S(2)}, u32[]{:S(2)}) collective-permute-start(bf16[2,192,640]{2,1,0:T(8,128)(2,1)} %dynamic-slice_bitcast_fusion.3), channel_id=1, source_target_pairs={{0,8},{4,12},{8,0},{12,4},{16,24},{20,28},{24,16},{28,20},{1,9},{5... | collective-permute-start | bytes 1474568 | tf_op jit(solution)/shard_map/ppermute | solution.py:95
  257.7 4.5 %copy-start.45 = (bf16[512,256]{1,0:T(8,128)(2,1)}, bf16[512,256]{1,0:T(8,128)(2,1)S(1)}, u32[]{:S(2)}) copy-start(bf16[512,256]{1,0:T(8,128)(2,1)S(1)} %get-tuple-element.120) | copy-start | bytes 786436
  262.5 4.7 %copy-start.14 = (bf16[512,640]{1,0:T(8,128)(2,1)S(1)}, bf16[512,640]{1,0:T(8,128)(2,1)}, u32[]{:S(2)}) copy-start(bf16[512,640]{1,0:T(8,128)(2,1)} %param.9) | copy-start | bytes 1966084
  262.5 4.6 %copy-start.33 = (bf16[512,1024]{1,0:T(8,128)(2,1)S(1)}, bf16[512,1024]{1,0:T(8,128)(2,1)}, u32[]{:S(2)}) copy-start(bf16[512,1024]{1,0:T(8,128)(2,1)} %get-tuple-element.104) | copy-start | bytes 3145732
  263.7 6.4 %collective-permute-start.8 = (bf16[2,2,2,2,48,640]{5,4,3,1,0,2:T(8,128)(2,1)}, bf16[2,2,2,2,48,640]{5,4,3,1,0,2:T(8,128)(2,1)}, u32[]{:S(2)}, u32[]{:S(2)}) collective-permute-start(bf16[2,2,2,2,48,640]{5,4,3,1,0,2:T(8,128)(2,1)} %pad_maximum_fusion.7), channel_id=1, source_target_pairs={{0,1},{1,0},{2,3},{3,2},{4,5},{5,4},{6,7},{7,6},{8,9},{9,8},{10,11... | collective-permute-start | bytes 2949128 | tf_op jit(solution)/shard_map/ppermute | solution.py:95
  265.7 32.6 %collective-permute-start.17 = (bf16[192,640]{1,0:T(8,128)(2,1)S(1)}, bf16[192,640]{1,0:T(8,128)(2,1)S(1)}, u32[]{:S(2)}, u32[]{:S(2)}) collective-permute-start(bf16[192,640]{1,0:T(8,128)(2,1)S(1)} %dynamic-slice_bitcast_fusion.7), channel_id=1, source_target_pairs={{0,16},{4,20},{8,24},{12,28},{16,0},{20,4},{24,8},{28,12},{1,17},{... | collective-permute-start | bytes 737288 | tf_op jit(solution)/shard_map/ppermute | solution.py:95
  270.0 5.0 %collective-permute-start.11 = (bf16[2,2,2,2,48,640]{5,4,0,1,2,3:T(8,128)(2,1)S(1)}, bf16[2,2,2,2,48,640]{5,4,0,1,2,3:T(8,128)(2,1)S(1)}, u32[]{:S(2)}, u32[]{:S(2)}) collective-permute-start(bf16[2,2,2,2,48,640]{5,4,0,1,2,3:T(8,128)(2,1)S(1)} %bitcast.289), channel_id=1, source_target_pairs={{0,1},{1,0},{2,3},{3,2},{4,5},{5,4},{6,7},{7,6},{8,9},{9,8},{10,11... | collective-permute-start | bytes 2949128 | tf_op jit(solution)/shard_map/ppermute | solution.py:95
  274.1 13.0 %collective-permute-start.9 = (bf16[2,2,2,48,640]{4,2,1,0,3:T(2,128)(2,1)S(1)}, bf16[2,2,2,48,640]{4,2,1,0,3:T(2,128)(2,1)S(1)}, u32[]{:S(2)}, u32[]{:S(2)}) collective-permute-start(bf16[2,2,2,48,640]{4,2,1,0,3:T(2,128)(2,1)S(1)} %pad_maximum_fusion.13), channel_id=1, source_target_pairs={{0,4},{4,0},{8,12},{12,8},{16,20},{20,16},{24,28},{28,24},{1,5},{5... | collective-permute-start | bytes 1474568 | tf_op jit(solution)/shard_map/ppermute | solution.py:95
  275.3 14.3 %collective-permute-start.12 = (bf16[2,2,2,48,640]{4,3,0,1,2:T(8,128)(2,1)S(1)}, bf16[2,2,2,48,640]{4,3,0,1,2:T(8,128)(2,1)S(1)}, u32[]{:S(2)}, u32[]{:S(2)}) collective-permute-start(bf16[2,2,2,48,640]{4,3,0,1,2:T(8,128)(2,1)S(1)} %dynamic-slice_bitcast_fusion.4), channel_id=1, source_target_pairs={{0,2},{1,3},{2,0},{3,1},{4,6},{5,7},{6,4},{7,5},{8,10},{9,11},{10,... | collective-permute-start | bytes 1474568 | tf_op jit(solution)/shard_map/ppermute | solution.py:95
  287.6 9.2 %copy-start.5 = (f32[512,640]{1,0:T(8,128)S(1)}, f32[512,640]{1,0:T(8,128)}, u32[]{:S(2)}) copy-start(f32[512,640]{1,0:T(8,128)} %copy-done.4) | copy-start | bytes 3932164
  287.6 9.2 %copy-start.24 = (f32[512,640]{1,0:T(8,128)S(1)}, f32[512,640]{1,0:T(8,128)}, u32[]{:S(2)}) copy-start(f32[512,640]{1,0:T(8,128)} %get-tuple-element.161) | copy-start | bytes 3932164
  287.6 7.0 %collective-permute-start.10 = (bf16[2,2,48,640]{3,2,1,0:T(8,128)(2,1)S(1)}, bf16[2,2,48,640]{3,2,1,0:T(8,128)(2,1)S(1)}, u32[]{:S(2)}, u32[]{:S(2)}) collective-permute-start(bf16[2,2,48,640]{3,2,1,0:T(8,128)(2,1)S(1)} %pad_maximum_fusion.14), channel_id=1, source_target_pairs={{0,2},{1,3},{2,0},{3,1},{4,6},{5,7},{6,4},{7,5},{8,10},{9,11},{10,... | collective-permute-start | bytes 737288 | tf_op jit(solution)/shard_map/ppermute | solution.py:95
  289.8 6.6 %collective-permute-start.13 = (bf16[2,2,48,640]{3,2,0,1:T(8,128)(2,1)S(1)}, bf16[2,2,48,640]{3,2,0,1:T(8,128)(2,1)S(1)}, u32[]{:S(2)}, u32[]{:S(2)}) collective-permute-start(bf16[2,2,48,640]{3,2,0,1:T(8,128)(2,1)S(1)} %dynamic-slice_bitcast_fusion.8), channel_id=1, source_target_pairs={{0,4},{4,0},{8,12},{12,8},{16,20},{20,16},{24,28},{28,24},{1,5},{5... | collective-permute-start | bytes 737288 | tf_op jit(solution)/shard_map/ppermute | solution.py:95
  296.5 6.3 %collective-permute-start.14 = (bf16[2,96,640]{2,1,0:T(8,128)(2,1)S(1)}, bf16[2,96,640]{2,1,0:T(8,128)(2,1)S(1)}, u32[]{:S(2)}, u32[]{:S(2)}) collective-permute-start(bf16[2,96,640]{2,1,0:T(8,128)(2,1)S(1)} %pad_maximum_fusion.15), channel_id=1, source_target_pairs={{0,8},{4,12},{8,0},{12,4},{16,24},{20,28},{24,16},{28,20},{1,9},{5... | collective-permute-start | bytes 737288 | tf_op jit(solution)/shard_map/ppermute | solution.py:95
  303.0 6.9 %collective-permute-start.15 = (bf16[96,640]{1,0:T(8,128)(2,1)S(1)}, bf16[96,640]{1,0:T(8,128)(2,1)S(1)}, u32[]{:S(2)}, u32[]{:S(2)}) collective-permute-start(bf16[96,640]{1,0:T(8,128)(2,1)S(1)} %pad_maximum_fusion.16), channel_id=1, source_target_pairs={{0,16},{4,20},{8,24},{12,28},{16,0},{20,4},{24,8},{28,12},{1,17},{... | collective-permute-start | bytes 368648 | tf_op jit(solution)/shard_map/ppermute | solution.py:95
  (62 other events, 145.7 us)

commit v2 on v1

--- a/solution.py
+++ b/solution.py
@@ -1,3 +1,5 @@
+import functools
+
 import jax
 import jax.numpy as jnp
 from jax import lax
@@ -99,15 +101,18 @@
     return (lax.axis_index(axis) >> bit) & 1
 
 
-def cut_rows(rows):
-    tiles = rows // 16
-    count = min(6, tiles)
-    edges = [tiles * k // count * 16 for k in range(count + 1)]
-    return [(edges[k], edges[k + 1] - edges[k]) for k in range(count)]
-
-
-def gather_kernel(pack_ref, full_ref, local_sem, send_sem, recv_sem):
-    far_size, _, high_size = full_ref.shape[:3]
+def cut_rows(row_counts):
+    chunks = []
+    for k, rows in enumerate(row_counts):
+        parts = 2 if rows % 32 == 0 and rows >= 64 else 1
+        chunks += [(k, p * rows // parts, rows // parts) for p in range(parts)]
+    return chunks
+
+
+def gather_kernel(count, *refs):
+    pack_refs, full_refs = refs[:count], refs[count : 2 * count]
+    local_sem, send_sem, recv_sem = refs[2 * count :]
+    far_size, _, high_size = full_refs[0].shape[:3]
     dp_at = lax.axis_index("dp")
     seq_at = lax.axis_index("seq")
     far, low = dp_at // 2, dp_at % 2
@@ -123,15 +128,15 @@
     for peer in peers:
         pl.semaphore_signal(barrier, inc=1, device_id=peer, device_id_type=pl.DeviceIdType.MESH)
     pl.semaphore_wait(barrier, len(peers))
-    chunks = cut_rows(pack_ref.shape[0])
+    chunks = cut_rows([ref.shape[0] for ref in pack_refs])
     every = slice(None)
 
     def copies(chunk, stage):
-        start, size = chunks[chunk]
+        which, start, size = chunks[chunk]
         rows = pl.ds(start, size)
         low_first = chunk % 2 == 0
         if stage == 0:
-            kind, src, place = 0, pack_ref.at[rows], (far, low, high, core)
+            kind, src, place = 0, pack_refs[which].at[rows], (far, low, high, core)
         elif stage == 3:
             kind, src, place = 3, None, (every, every, every, core)
         elif stage == 1:
@@ -140,7 +145,7 @@
             kind, src, place = 2, None, (every, every, high, core)
         else:
             kind, src, place = 1, None, (every, low, every, core)
-        target = full_ref.at[place + (rows,)]
+        target = full_refs[which].at[place + (rows,)]
         return [
             pltpu.make_async_remote_copy(
                 src_ref=target if src is None else src,
@@ -153,12 +158,21 @@
             for k, peer in enumerate(groups[kind])
         ]
 
-    for chunk in range(len(chunks)):
-        for copy in copies(chunk, 0):
-            copy.start()
-    own = pltpu.make_async_copy(pack_ref, full_ref.at[far, low, high, core], local_sem)
-    own.start()
-    own.wait()
+    def launch(pair):
+        for chunk in (2 * pair, 2 * pair + 1):
+            if chunk < len(chunks):
+                for copy in copies(chunk, 0):
+                    copy.start()
+
+    launch(0)
+    own = [
+        pltpu.make_async_copy(pack_refs[k], full_refs[k].at[far, low, high, core], local_sem.at[k])
+        for k in range(count)
+    ]
+    for copy in own:
+        copy.start()
+    for copy in own:
+        copy.wait()
     for turn in range((len(chunks) + 1) // 2 + 3):
         for stage in range(4):
             for chunk in (2 * (turn - stage), 2 * (turn - stage) + 1):
@@ -168,30 +182,36 @@
                     if stage < 3:
                         for copy in copies(chunk, stage + 1):
                             copy.start()
+                if stage == 0 and chunk % 2 == 1:
+                    launch(turn + 1)
     for chunk in range(len(chunks)):
         for stage in range(4):
             for copy in copies(chunk, stage):
                 copy.wait_send()
 
 
-def gather_rows(pack):
+def gather_rows(packs):
     far_size = lax.axis_size("dp") // 2
     high_size = lax.axis_size("seq") // 2
-    chunk_count = len(cut_rows(pack.shape[0]))
+    packs = [jnp.pad(pack, ((0, -pack.shape[0] % 16), (0, 0))) for pack in packs]
+    chunk_count = len(cut_rows([pack.shape[0] for pack in packs]))
     sem_count = far_size + high_size
-    full = pl.pallas_call(
-        gather_kernel,
-        out_shape=jax.ShapeDtypeStruct((far_size, 2, high_size, 2) + pack.shape, pack.dtype),
-        in_specs=[pl.BlockSpec(memory_space=pl.ANY)],
-        out_specs=pl.BlockSpec(memory_space=pl.ANY),
+    fulls = pl.pallas_call(
+        functools.partial(gather_kernel, len(packs)),
+        out_shape=[
+            jax.ShapeDtypeStruct((far_size, 2, high_size, 2) + pack.shape, pack.dtype)
+            for pack in packs
+        ],
+        in_specs=[pl.BlockSpec(memory_space=pl.ANY)] * len(packs),
+        out_specs=[pl.BlockSpec(memory_space=pl.ANY)] * len(packs),
         scratch_shapes=[
-            pltpu.SemaphoreType.DMA,
+            pltpu.SemaphoreType.DMA((len(packs),)),
             pltpu.SemaphoreType.DMA((chunk_count, sem_count)),
             pltpu.SemaphoreType.DMA((chunk_count, sem_count)),
         ],
         compiler_params=pltpu.CompilerParams(collective_id=0, has_side_effects=True),
-    )(pack)
-    return full.reshape((-1,) + pack.shape)
+    )(*packs)
+    return [full.reshape((-1,) + pack.shape) for full, pack in zip(fulls, packs)]
 
 
 def pack_exact(values):
@@ -271,27 +291,14 @@
     out_rows = w_out.shape[0]
     gate_up_rows = w_gate_up.shape[1]
     gain_row = jnp.pad(norm_gains.reshape(1, gain_len), ((0, 0), (0, D - gain_len)))
-    lead_rows = qkv_rows + out_rows
-    lead_pad = -(lead_rows + 1) % 16
-    ffn_start = lead_rows + 1 + lead_pad
-    pack = jnp.concatenate(
-        [
-            w_qkv.T,
-            w_out,
-            jnp.pad(gain_row, ((0, lead_pad), (0, 0))),
-            w_gate_up.T,
-            w_down,
-        ],
-        0,
-    )
-    pack = jnp.pad(pack, ((0, -pack.shape[0] % 16), (0, 0)))
-    full = gather_rows(pack)
-    qkv_full = full[:, :qkv_rows].reshape(-1, D)
-    out_full = full[:, qkv_rows:lead_rows].reshape(-1, D)
-    gain_parts = full[:, lead_rows, :gain_len].reshape(-1)
-    down_start = ffn_start + gate_up_rows
-    gate_up_full = full[:, ffn_start:down_start].reshape(-1, D)
-    down_full = full[:, down_start : down_start + w_down.shape[0]].reshape(-1, D)
+    qkv_full, out_full, gate_up_full, down_full, gain_full = gather_rows(
+        [w_qkv.T, w_out, w_gate_up.T, w_down, gain_row]
+    )
+    qkv_full = qkv_full[:, :qkv_rows].reshape(-1, D)
+    out_full = out_full[:, :out_rows].reshape(-1, D)
+    gate_up_full = gate_up_full[:, :gate_up_rows].reshape(-1, D)
+    down_full = down_full[:, : w_down.shape[0]].reshape(-1, D)
+    gain_parts = gain_full[:, 0, :gain_len].reshape(-1)
     gain_in, gain_attn_post, gain_ffn_pre, gain_ffn_post, gain_query, gain_key = split_gains(
         gain_parts.astype(jnp.float32)
     )

time: 317 us -> 308 us (0.972)
  local copies, waits for them, and re-layouts: 56.4 us -> 43.1 us
    slice x4 -> x0, local copies, waits for them, and re-layouts: 13.5 us -> none  [the longest x1 5.72 us: body(): gate_up_full = full[:, ffn_start:down_start].reshape(-1, D)]
    unnamed x171 -> x161, local copies, waits for them, and re-layouts: 15.1 us -> 16.8 us
  transfers between devices with their start and end apart: 18 -> 18, of which waited for: 9 -> 8; matrix products, arithmetic and copies ran while one was open for 29% -> 26% of each run, Pallas kernels for 0% -> 0%
where the time goes in v2:
time: 308 us; the launch traced here: 304 us
  Pallas kernels  80.6 us (26%)
  matrix products  59.7 us (19%)
  waiting for transfers between devices  48.8 us (16%)
  other arithmetic  46.9 us (15%)
  local copies, waits for them, and re-layouts  43.1 us (14%)
  starting transfers between devices  22.3 us (7%)
    pallas_call x1, Pallas kernels, gather_rows(): pl.pallas_call(functools.partial(gather_kernel, len(packs)), out_shape=[j...  80.6 us
    ppermute x16, waiting for transfers between devices, swap(): return lax.ppermute(block, axis, route)  48.8 us
    ppermute x16, starting transfers between devices, swap(): return lax.ppermute(block, axis, route)  17.5 us
    unnamed x161, local copies, waits for them, and re-layouts  16.8 us
    sub x1, matrix products, body(): grad_scores = (probs * (grad_probs - inner_sum)).astype(jnp.bfloat16)  12.5 us
    convert_element_type x14, other arithmetic, scatter_steps(): block = block.astype(jnp.bfloat16)  8.66 us
    dot_general x1, matrix products, body(): jnp.einsum('hqk,qhd->kd', probs_again, grad_attended, preferred_element_t...  6.39 us
  transfers between devices with their start and end apart: 18, of which 8 were waited for; matrix products, arithmetic and copies ran while one was open for 26% of the time, Pallas kernels for 0%

profile of v2, /device:TPU:0, one launch (start us, length us, event | category | flops | bytes accessed | tf_op | source)
XLA Modules:
  0.0 303.8 jit_solution(15171375787133139678)
XLA Ops:
  3.6 80.6 %shard_map.144 = (bf16[4,2,2,2,48,640]{5,4,3,2,1,0:T(8,128)(2,1)}, bf16[4,2,2,2,32,640]{5,4,3,2,1,0:T(8,128)(2,1)}, bf16[4,2,2,2,128,640]{5,4,3,2,1,0:T(8,128)(2...) custom-call(bf16[48,640]{1,0:T(8,128)(2,1)} %bitcast.275, bf16[32,640]{1,0:T(8,128)(2,1)} %refs_1_.1, ...), custom_call_target="tpu_custom_call" | custom-call | tf_op jit(solution)/shard_map/pallas_call | solution.py:199
  88.2 3.2 %fusion.94 = f32[512,1536]{1,0:T(8,128)S(1)} fusion(bf16[1536,640]{1,0:T(8,128)(2,1)} %bitcast.297, bf16[512,640]{1,0:T(8,128)(2,1)} %param.9, f32[640]{0:T(1024)S(1)} %get-tuple-element.142, f32[512]{0:T(512)S(1)} %add_rsqrt_fusion.5), kind=kOutput, calls=%fused_computation.203 | convolution fusion | flops 1007943680 | bytes 5771776 | tf_op jit(solution)/shard_map/rd,cd->rc/dot_general | solution.py:314
  93.9 2.5 multiply_cosine_fusion
  97.2 3.3 %collective-permute-start = (bf16[512,512]{1,0:T(8,128)(2,1)}, bf16[512,512]{1,0:T(8,128)(2,1)}, u32[]{:S(2)}, u32[]{:S(2)}) collective-permute-start(bf16[512,512]{1,0:T(8,128)(2,1)} %pad_maximum_fusion.10), channel_id=1, source_target_pairs={{0,1},{1,2},{2,3},{4,5},{5,6},{6,7},{8,9},{9,10},{10,11},{12,13},{... | collective-permute-start | bytes 1572872 | tf_op jit(solution)/shard_map/ppermute | solution.py:24
  102.3 2.0 reshape.459
  104.3 2.2 multiply_reduce_fusion.2
  119.2 2.7 copy-done.5
  121.9 2.7 fusion.37
  126.5 3.5 %fusion.155 = f32[512,4096]{1,0:T(8,128)S(1)} fusion(bf16[4096,640]{1,0:T(8,128)(2,1)S(1)} %bitcast.293, f32[512,640]{1,0:T(8,128)S(1)} %get-tuple-element.110, f32[640]{0:T(1024)S(1)} %get-tuple-element.140, f32[512]{0:T(512)S(1)} %add_rsqrt_fusion.2), kind=kOutput, calls=%fused_computation.337 | convolution fusion | flops 2685337600 | bytes 14946816 | tf_op jit(solution)/shard_map/rd,fd->rf/dot_general | solution.py:372
  130.0 1.9 multiply_convert_fusion.1
  136.2 4.6 %fusion.14 = (bf16[512,2048]{1,0:T(8,128)(2,1)S(1)}, bf16[512,2048]{1,0:T(8,128)(2,1)S(1)}) fusion(f32[512,4096]{1,0:T(8,128)S(1)} %fusion.155, bf16[512,640]{1,0:T(8,128)(2,1)S(1)} %get-tuple-element.125, bf16[2048,640]{1,0:T(8,128)(2,1)S(1)} %bitcast.296), kind=kOutput, calls=%fused_computation.22 | convolution fusion | flops 1367343104 | bytes 15859712 | tf_op jit(solution)/shard_map/rd,fd->rf/dot_general | solution.py:387
  142.8 3.5 %fusion.21 = f32[512,640]{1,0:T(8,128)S(1)} fusion(bf16[4096,640]{1,0:T(8,128)(2,1)S(1)} %bitcast.294, bf16[512,2048]{1,0:T(8,128)(2,1)S(1)} %get-tuple-element.112, bf16[512,2048]{1,0:T(8,128)(2,1)S(1)} %get-tuple-element.111), kind=kOutput, calls=%fused_computation.40 | convolution fusion | flops 2692743168 | bytes 10747904 | tf_op jit(solution)/shard_map/dot_general | solution.py:396
  146.3 5.8 %convolution_convert_fusion = bf16[4096,640]{1,0:T(8,128)(2,1)S(1)} fusion(bf16[512,2048]{1,0:T(8,128)(2,1)} %copy-done.70, bf16[512,2048]{1,0:T(8,128)(2,1)} %copy-done.69, f32[512,640]{1,0:T(8,128)S(1)} %get-tuple-element.110, f32[640]{0:T(1024)S(1)} %get-tuple-element.140, f32[512]{0:T(512)S(1)} %add_rsqrt_fusion.2), kind=kOutput, calls=%fused_computation.11 | convolution fusion | flops 2696347648 | bytes 10752512 | tf_op jit(solution)/shard_map/rf,rd->fd/dot_general | solution.py:392
  165.2 2.1 convolution_convert_fusion.4
  167.2 2.4 copy.302
  169.7 6.4 %fusion.38 = f32[1024,256]{1,0:T(8,128)} fusion(bf16[512,4,256]{0,2,1:T(8,128)(2,1)} %bitcast.270, f32[1024,512,4]{1,0,2:T(8,128)} %copy-done.5, f32[4,512]{1,0:T(4,128)S(1)} %copy-done.58, pred[512,1024]{0,1:T(8,128)(4,1)S(1)} %fusion.24), kind=kOutput, calls=%fused_computation.80 | convolution fusion | flops 1080033280 | bytes 11018240 | tf_op jit(solution)/shard_map/hqk,qhd->kd/dot_general | solution.py:427
  176.1 12.5 %fusion.2 = bf16[4,512,1024]{1,2,0:T(8,128)(2,1)} fusion(f32[1024,512,4]{1,0,2:T(8,128)} %copy-done.5, f32[4,512]{1,0:T(4,128)S(1)} %copy-done.58, pred[512,1024]{0,1:T(8,128)(4,1)S(1)} %fusion.24, bf16[512,4,256]{0,2,1:T(8,128)(2,1)} %bitcast.271, bf16[512,256]{1,0:T(8,128)(2,1)S(1)} %copy-done.20, bf16[512,256]{1,0:T(8,128)(2,1)} %copy-done.35), kind=kOutput, calls=%fused_computation.4 | convolution fusion | flops 2166361088 | bytes 14688256 | tf_op jit(solution)/shard_map/sub | solution.py:431
  188.6 2.8 fusion.20
  191.4 2.1 fusion.19
  193.8 2.3 collective-permute-start.5
  201.5 15.8 %collective-permute-done.3 = bf16[2,2,2,96,640]{4,3,2,1,0:T(8,128)(2,1)S(1)} collective-permute-done((bf16[2,2,2,96,640]{4,3,2,1,0:T(8,128)(2,1)S(1)}, bf16[2,2,2,96,640]{4,3,2,1,0:T(8,128)(2,1)S(1)}, u32[]{:S(2)}, u32[]{:S(2)}) %collective-permute-start.3) | collective-permute-done | bytes 983072 | tf_op jit(solution)/shard_map/ppermute | solution.py:97
  217.7 2.3 collective-permute-start.4
  222.5 8.0 %collective-permute-done.4 = bf16[2,2,96,640]{3,2,1,0:T(8,128)(2,1)S(1)} collective-permute-done((bf16[2,2,96,640]{3,2,1,0:T(8,128)(2,1)S(1)}, bf16[2,2,96,640]{3,2,1,0:T(8,128)(2,1)S(1)}, u32[]{:S(2)}, u32[]{:S(2)}) %collective-permute-start.4) | collective-permute-done | bytes 491552 | tf_op jit(solution)/shard_map/ppermute | solution.py:97
  233.8 2.3 collective-permute-start.16
  245.1 2.1 multiply_reduce_fusion
  251.8 2.5 fusion.49
  259.7 2.5 convolution_convert_fusion.2
  269.2 10.3 %collective-permute-done.9 = bf16[2,2,2,48,640]{4,2,1,0,3:T(2,128)(2,1)S(1)} collective-permute-done((bf16[2,2,2,48,640]{4,2,1,0,3:T(2,128)(2,1)S(1)}, bf16[2,2,2,48,640]{4,2,1,0,3:T(2,128)(2,1)S(1)}, u32[]{:S(2)}, u32[]{:S(2)}) %collective-permute-start.9) | collective-permute-done | bytes 491552 | tf_op jit(solution)/shard_map/ppermute | solution.py:97
  282.7 4.3 %collective-permute-done.10 = bf16[2,2,48,640]{3,2,1,0:T(8,128)(2,1)S(1)} collective-permute-done((bf16[2,2,48,640]{3,2,1,0:T(8,128)(2,1)S(1)}, bf16[2,2,48,640]{3,2,1,0:T(8,128)(2,1)S(1)}, u32[]{:S(2)}, u32[]{:S(2)}) %collective-permute-start.10) | collective-permute-done | bytes 245792 | tf_op jit(solution)/shard_map/ppermute | solution.py:97
  290.9 4.0 %collective-permute-done.14 = bf16[2,96,640]{2,1,0:T(8,128)(2,1)S(1)} collective-permute-done((bf16[2,96,640]{2,1,0:T(8,128)(2,1)S(1)}, bf16[2,96,640]{2,1,0:T(8,128)(2,1)S(1)}, u32[]{:S(2)}, u32[]{:S(2)}) %collective-permute-start.14) | collective-permute-done | bytes 245792 | tf_op jit(solution)/shard_map/ppermute | solution.py:97
  295.1 2.2 collective-permute-start.15
  298.2 3.5 %collective-permute-done.15 = bf16[96,640]{1,0:T(8,128)(2,1)S(1)} collective-permute-done((bf16[96,640]{1,0:T(8,128)(2,1)S(1)}, bf16[96,640]{1,0:T(8,128)(2,1)S(1)}, u32[]{:S(2)}, u32[]{:S(2)}) %collective-permute-start.15) | collective-permute-done | bytes 122912 | tf_op jit(solution)/shard_map/ppermute | solution.py:97
  (326 shorter events, 92.7 us)
Async XLA Ops:
  85.8 5.7 %copy-start.49 = (f32[640]{0:T(1024)}, f32[640]{0:T(1024)S(1)}, u32[]{:S(2)}) copy-start(f32[640]{0:T(1024)S(1)} %get-tuple-element.142) | copy-start | bytes 7684
  86.4 6.8 %copy-start.51 = (f32[256]{0:T(256)}, f32[256]{0:T(256)S(1)}, u32[]{:S(2)}) copy-start(f32[256]{0:T(256)S(1)} %get-tuple-element.144) | copy-start | bytes 3076
  91.5 5.7 %copy-start.1 = (f32[512,1536]{1,0:T(8,128)}, f32[512,1536]{1,0:T(8,128)S(1)}, u32[]{:S(2)}) copy-start(f32[512,1536]{1,0:T(8,128)S(1)} %fusion.94) | copy-start | bytes 9437188
  93.1 9.1 %copy-start.43 = (f32[512]{0:T(512)}, f32[512]{0:T(512)S(1)}, u32[]{:S(2)}) copy-start(f32[512]{0:T(512)S(1)} %convert_element_type.363) | copy-start | bytes 6148
  97.2 17.4 %collective-permute-start = (bf16[512,512]{1,0:T(8,128)(2,1)}, bf16[512,512]{1,0:T(8,128)(2,1)}, u32[]{:S(2)}, u32[]{:S(2)}) collective-permute-start(bf16[512,512]{1,0:T(8,128)(2,1)} %pad_maximum_fusion.10), channel_id=1, source_target_pairs={{0,1},{1,2},{2,3},{4,5},{5,6},{6,7},{8,9},{9,10},{10,11},{12,13},{... | collective-permute-start | bytes 1572872 | tf_op jit(solution)/shard_map/ppermute | solution.py:24
  117.6 8.9 %slice-start = ((s8[5242880]{0:T(1024)(128)(4,1)}), s8[4194304]{0:T(1024)(128)(4,1)S(1)}, s32[]{:S(2)}) async-start(s8[5242880]{0:T(1024)(128)(4,1)} %bitcast.291), calls=%async_computation | async-start | bytes 8388608
  121.9 4.6 %slice-start.1 = ((s8[5242880]{0:T(1024)(128)(4,1)}), s8[1048576]{0:T(1024)(128)(4,1)S(1)}, s32[]{:S(2)}) async-start(s8[5242880]{0:T(1024)(128)(4,1)} %bitcast.291), calls=%async_computation.1 | async-start | bytes 2097152
  154.5 4.4 %copy-start = (bf16[32,96,640]{2,1,0:T(8,128)(2,1)}, bf16[32,96,640]{2,1,0:T(8,128)(2,1)S(1)}, u32[]{:S(2)}) copy-start(bf16[32,96,640]{2,1,0:T(8,128)(2,1)S(1)} %slice.195) | copy-start | bytes 11796484
  158.9 32.5 %collective-permute-start.2 = (bf16[2,2,2,2,96,640]{5,4,1,0,3,2:T(8,128)(2,1)}, bf16[2,2,2,2,96,640]{5,4,1,0,3,2:T(8,128)(2,1)}, u32[]{:S(2)}, u32[]{:S(2)}) collective-permute-start(bf16[2,2,2,2,96,640]{5,4,1,0,3,2:T(8,128)(2,1)} %bitcast.246), channel_id=1, source_target_pairs={{0,1},{1,0},{2,3},{3,2},{4,5},{5,4},{6,7},{7,6},{8,9},{9,8},{10,11... | collective-permute-start | bytes 5898248 | tf_op jit(solution)/shard_map/ppermute | solution.py:97
  160.4 28.2 %collective-permute-start.1 = (bf16[2,2,2,2,96,640]{5,4,3,2,1,0:T(8,128)(2,1)}, bf16[2,2,2,2,96,640]{5,4,3,2,1,0:T(8,128)(2,1)}, u32[]{:S(2)}, u32[]{:S(2)}) collective-permute-start(bf16[2,2,2,2,96,640]{5,4,3,2,1,0:T(8,128)(2,1)} %dynamic-slice_bitcast_fusion), channel_id=1, source_target_pairs={{0,1},{1,0},{2,3},{3,2},{4,5},{5,4},{6,7},{7,6},{8,9},{9,8},{10,11... | collective-permute-start | bytes 5898248 | tf_op jit(solution)/shard_map/ppermute | solution.py:97
  165.2 4.5 %copy-start.58 = (f32[4,512]{1,0:T(4,128)S(1)}, f32[4,512]{1,0:T(4,128)}, u32[]{:S(2)}) copy-start(f32[4,512]{1,0:T(4,128)} %log_add_fusion) | copy-start | bytes 24580
  193.6 23.7 %collective-permute-start.3 = (bf16[2,2,2,96,640]{4,3,2,1,0:T(8,128)(2,1)S(1)}, bf16[2,2,2,96,640]{4,3,2,1,0:T(8,128)(2,1)S(1)}, u32[]{:S(2)}, u32[]{:S(2)}) collective-permute-start(bf16[2,2,2,96,640]{4,3,2,1,0:T(8,128)(2,1)S(1)} %dynamic-slice_bitcast_fusion.2), channel_id=1, source_target_pairs={{0,2},{1,3},{2,0},{3,1},{4,6},{5,7},{6,4},{7,5},{8,10},{9,11},{10,... | collective-permute-start | bytes 2949128 | tf_op jit(solution)/shard_map/ppermute | solution.py:97
  193.8 26.2 %collective-permute-start.5 = (bf16[2,2,2,96,640]{4,3,1,0,2:T(8,128)(2,1)S(1)}, bf16[2,2,2,96,640]{4,3,1,0,2:T(8,128)(2,1)S(1)}, u32[]{:S(2)}, u32[]{:S(2)}) collective-permute-start(bf16[2,2,2,96,640]{4,3,1,0,2:T(8,128)(2,1)S(1)} %dynamic-slice_bitcast_fusion.1), channel_id=1, source_target_pairs={{0,4},{4,0},{8,12},{12,8},{16,20},{20,16},{24,28},{28,24},{1,5},{5... | collective-permute-start | bytes 2949128 | tf_op jit(solution)/shard_map/ppermute | solution.py:97
  201.5 35.0 %copy-start.29 = (f32[1024,256]{1,0:T(8,128)}, f32[1024,256]{1,0:T(8,128)S(1)}, u32[]{:S(2)}) copy-start(f32[1024,256]{1,0:T(8,128)S(1)} %convolution_bitcast_fusion.1) | copy-start | bytes 3145732
  217.7 12.8 %collective-permute-start.4 = (bf16[2,2,96,640]{3,2,1,0:T(8,128)(2,1)S(1)}, bf16[2,2,96,640]{3,2,1,0:T(8,128)(2,1)S(1)}, u32[]{:S(2)}, u32[]{:S(2)}) collective-permute-start(bf16[2,2,96,640]{3,2,1,0:T(8,128)(2,1)S(1)} %dynamic-slice_bitcast_fusion.6), channel_id=1, source_target_pairs={{0,4},{4,0},{8,12},{12,8},{16,20},{20,16},{24,28},{28,24},{1,5},{5... | collective-permute-start | bytes 1474568 | tf_op jit(solution)/shard_map/ppermute | solution.py:97
  220.3 12.1 %collective-permute-start.6 = (bf16[2,2,96,640]{3,2,1,0:T(8,128)(2,1)S(1)}, bf16[2,2,96,640]{3,2,1,0:T(8,128)(2,1)S(1)}, u32[]{:S(2)}, u32[]{:S(2)}) collective-permute-start(bf16[2,2,96,640]{3,2,1,0:T(8,128)(2,1)S(1)} %dynamic-slice_bitcast_fusion.5), channel_id=1, source_target_pairs={{0,2},{1,3},{2,0},{3,1},{4,6},{5,7},{6,4},{7,5},{8,10},{9,11},{10,... | collective-permute-start | bytes 1474568 | tf_op jit(solution)/shard_map/ppermute | solution.py:97
  233.8 23.2 %collective-permute-start.16 = (bf16[2,192,640]{2,1,0:T(8,128)(2,1)}, bf16[2,192,640]{2,1,0:T(8,128)(2,1)}, u32[]{:S(2)}, u32[]{:S(2)}) collective-permute-start(bf16[2,192,640]{2,1,0:T(8,128)(2,1)} %dynamic-slice_bitcast_fusion.3), channel_id=1, source_target_pairs={{0,8},{4,12},{8,0},{12,4},{16,24},{20,28},{24,16},{28,20},{1,9},{5... | collective-permute-start | bytes 1474568 | tf_op jit(solution)/shard_map/ppermute | solution.py:97
  237.4 9.9 %collective-permute-start.7 = (bf16[512,512]{1,0:T(8,128)(2,1)}, bf16[512,512]{1,0:T(8,128)(2,1)}, u32[]{:S(2)}, u32[]{:S(2)}) collective-permute-start(bf16[512,512]{1,0:T(8,128)(2,1)} %pad_maximum_fusion.11), channel_id=1, source_target_pairs={{1,0},{2,1},{3,2},{5,4},{6,5},{7,6},{9,8},{10,9},{11,10},{13,12},{... | collective-permute-start | bytes 1572872 | tf_op jit(solution)/shard_map/ppermute | solution.py:24
  250.0 4.4 %copy-start.37 = (bf16[512,256]{1,0:T(8,128)(2,1)}, bf16[512,256]{1,0:T(8,128)(2,1)S(1)}, u32[]{:S(2)}) copy-start(bf16[512,256]{1,0:T(8,128)(2,1)S(1)} %get-tuple-element.130) | copy-start | bytes 786436
  254.6 5.1 %copy-start.12 = (bf16[512,640]{1,0:T(8,128)(2,1)S(1)}, bf16[512,640]{1,0:T(8,128)(2,1)}, u32[]{:S(2)}) copy-start(bf16[512,640]{1,0:T(8,128)(2,1)} %param.9) | copy-start | bytes 1966084
  254.6 5.0 %copy-start.26 = (bf16[512,1024]{1,0:T(8,128)(2,1)S(1)}, bf16[512,1024]{1,0:T(8,128)(2,1)}, u32[]{:S(2)}) copy-start(bf16[512,1024]{1,0:T(8,128)(2,1)} %get-tuple-element.114) | copy-start | bytes 3145732
  255.8 6.8 %collective-permute-start.8 = (bf16[2,2,2,2,48,640]{5,4,3,1,0,2:T(8,128)(2,1)}, bf16[2,2,2,2,48,640]{5,4,3,1,0,2:T(8,128)(2,1)}, u32[]{:S(2)}, u32[]{:S(2)}) collective-permute-start(bf16[2,2,2,2,48,640]{5,4,3,1,0,2:T(8,128)(2,1)} %pad_maximum_fusion.7), channel_id=1, source_target_pairs={{0,1},{1,0},{2,3},{3,2},{4,5},{5,4},{6,7},{7,6},{8,9},{9,8},{10,11... | collective-permute-start | bytes 2949128 | tf_op jit(solution)/shard_map/ppermute | solution.py:97
  258.2 32.0 %collective-permute-start.17 = (bf16[192,640]{1,0:T(8,128)(2,1)S(1)}, bf16[192,640]{1,0:T(8,128)(2,1)S(1)}, u32[]{:S(2)}, u32[]{:S(2)}) collective-permute-start(bf16[192,640]{1,0:T(8,128)(2,1)S(1)} %dynamic-slice_bitcast_fusion.7), channel_id=1, source_target_pairs={{0,16},{4,20},{8,24},{12,28},{16,0},{20,4},{24,8},{28,12},{1,17},{... | collective-permute-start | bytes 737288 | tf_op jit(solution)/shard_map/ppermute | solution.py:97
  262.5 4.7 %collective-permute-start.11 = (bf16[2,2,2,2,48,640]{5,4,0,1,2,3:T(8,128)(2,1)S(1)}, bf16[2,2,2,2,48,640]{5,4,0,1,2,3:T(8,128)(2,1)S(1)}, u32[]{:S(2)}, u32[]{:S(2)}) collective-permute-start(bf16[2,2,2,2,48,640]{5,4,0,1,2,3:T(8,128)(2,1)S(1)} %bitcast.272), channel_id=1, source_target_pairs={{0,1},{1,0},{2,3},{3,2},{4,5},{5,4},{6,7},{7,6},{8,9},{9,8},{10,11... | collective-permute-start | bytes 2949128 | tf_op jit(solution)/shard_map/ppermute | solution.py:97
  266.6 13.0 %collective-permute-start.9 = (bf16[2,2,2,48,640]{4,2,1,0,3:T(2,128)(2,1)S(1)}, bf16[2,2,2,48,640]{4,2,1,0,3:T(2,128)(2,1)S(1)}, u32[]{:S(2)}, u32[]{:S(2)}) collective-permute-start(bf16[2,2,2,48,640]{4,2,1,0,3:T(2,128)(2,1)S(1)} %pad_maximum_fusion.13), channel_id=1, source_target_pairs={{0,4},{4,0},{8,12},{12,8},{16,20},{20,16},{24,28},{28,24},{1,5},{5... | collective-permute-start | bytes 1474568 | tf_op jit(solution)/shard_map/ppermute | solution.py:97
  267.5 14.1 %collective-permute-start.12 = (bf16[2,2,2,48,640]{4,3,0,1,2:T(8,128)(2,1)S(1)}, bf16[2,2,2,48,640]{4,3,0,1,2:T(8,128)(2,1)S(1)}, u32[]{:S(2)}, u32[]{:S(2)}) collective-permute-start(bf16[2,2,2,48,640]{4,3,0,1,2:T(8,128)(2,1)S(1)} %dynamic-slice_bitcast_fusion.4), channel_id=1, source_target_pairs={{0,2},{1,3},{2,0},{3,1},{4,6},{5,7},{6,4},{7,5},{8,10},{9,11},{10,... | collective-permute-start | bytes 1474568 | tf_op jit(solution)/shard_map/ppermute | solution.py:97
  280.1 8.5 %copy-start.4 = (f32[512,640]{1,0:T(8,128)S(1)}, f32[512,640]{1,0:T(8,128)}, u32[]{:S(2)}) copy-start(f32[512,640]{1,0:T(8,128)} %copy-done.3) | copy-start | bytes 3932164
  280.1 8.5 %copy-start.18 = (f32[512,640]{1,0:T(8,128)S(1)}, f32[512,640]{1,0:T(8,128)}, u32[]{:S(2)}) copy-start(f32[512,640]{1,0:T(8,128)} %get-tuple-element.171) | copy-start | bytes 3932164
  280.1 6.8 %collective-permute-start.10 = (bf16[2,2,48,640]{3,2,1,0:T(8,128)(2,1)S(1)}, bf16[2,2,48,640]{3,2,1,0:T(8,128)(2,1)S(1)}, u32[]{:S(2)}, u32[]{:S(2)}) collective-permute-start(bf16[2,2,48,640]{3,2,1,0:T(8,128)(2,1)S(1)} %pad_maximum_fusion.14), channel_id=1, source_target_pairs={{0,2},{1,3},{2,0},{3,1},{4,6},{5,7},{6,4},{7,5},{8,10},{9,11},{10,... | collective-permute-start | bytes 737288 | tf_op jit(solution)/shard_map/ppermute | solution.py:97
  281.8 6.6 %collective-permute-start.13 = (bf16[2,2,48,640]{3,2,0,1:T(8,128)(2,1)S(1)}, bf16[2,2,48,640]{3,2,0,1:T(8,128)(2,1)S(1)}, u32[]{:S(2)}, u32[]{:S(2)}) collective-permute-start(bf16[2,2,48,640]{3,2,0,1:T(8,128)(2,1)S(1)} %dynamic-slice_bitcast_fusion.8), channel_id=1, source_target_pairs={{0,4},{4,0},{8,12},{12,8},{16,20},{20,16},{24,28},{28,24},{1,5},{5... | collective-permute-start | bytes 737288 | tf_op jit(solution)/shard_map/ppermute | solution.py:97
  288.5 6.3 %collective-permute-start.14 = (bf16[2,96,640]{2,1,0:T(8,128)(2,1)S(1)}, bf16[2,96,640]{2,1,0:T(8,128)(2,1)S(1)}, u32[]{:S(2)}, u32[]{:S(2)}) collective-permute-start(bf16[2,96,640]{2,1,0:T(8,128)(2,1)S(1)} %pad_maximum_fusion.15), channel_id=1, source_target_pairs={{0,8},{4,12},{8,0},{12,4},{16,24},{20,28},{24,16},{28,20},{1,9},{5... | collective-permute-start | bytes 737288 | tf_op jit(solution)/shard_map/ppermute | solution.py:97
  295.1 6.6 %collective-permute-start.15 = (bf16[96,640]{1,0:T(8,128)(2,1)S(1)}, bf16[96,640]{1,0:T(8,128)(2,1)S(1)}, u32[]{:S(2)}, u32[]{:S(2)}) collective-permute-start(bf16[96,640]{1,0:T(8,128)(2,1)S(1)} %pad_maximum_fusion.16), channel_id=1, source_target_pairs={{0,16},{4,20},{8,24},{12,28},{16,0},{20,4},{24,8},{28,12},{1,17},{... | collective-permute-start | bytes 368648 | tf_op jit(solution)/shard_map/ppermute | solution.py:97
  (59 other events, 139.6 us)
